TPU v7x, 512 devices: a whole 4x4x16 slice. The times are simulated.
512 devices in a mesh: dp: 32 (over x_lo, z), tensor: 16 (over y, x_hi, core).
Axes of the slice: x: 4 (x_hi: 2, x_lo: 2; x = x_hi * 2 + x_lo), y: 4, z: 16, core: 2. Of those that a mesh axis runs over, the one named last changes fastest.
Arguments:
- learn_acts: bfloat16 [16384, 8192], P('dp', 'tensor'), may hold values from -6 to 6
- cotangent: bfloat16 [16384, 1024], P('dp'), may hold values from -6 to 6
- base_weight: bfloat16 [8192, 1024], P('tensor'), may hold values from -0.0625 to 0.0625
- down_factor: float32 [64, 8192], P(None, 'tensor'), may hold values from -0.0625 to 0.0625
- up_factor: float32 [1024, 64], replicated, may hold values from -0.75 to 0.75
- decode_acts: bfloat16 [16384, 8192], P('dp', 'tensor'), may hold values from -6 to 6
Outputs:
- grad_acts: bfloat16 [16384, 8192], P('dp', 'tensor')
- new_down: float32 [64, 8192], P('dp', 'tensor')
- new_up: float32 [1024, 64], P(('dp', 'tensor'))
- decoded: bfloat16 [16384, 1024], P('dp')
All inputs are finite; a program needn't handle non-finite values.
Results may differ from a plain program's by a relative error of at most 0.025.
Values may be sent and summed in bfloat16 or wider, within the bound.
A program may use at most 64 MiB of HBM per device.

v0:
```python
import jax
import jax.numpy as jnp
from jax import lax
from jax.sharding import PartitionSpec as P

rate_down = 0.2
rate_up = 3.0


def update(old, summed, rate, total):
    return old - rate * (summed / total)


def body(learn_acts, cotangent, base_weight, down_factor, up_factor, decode_acts):
    n_data = lax.axis_size("dp")
    n_tensor = lax.axis_size("tensor")
    data_index = lax.axis_index("dp")
    tensor_index = lax.axis_index("tensor")
    local_tok = learn_acts.shape[0]
    total = local_tok * n_data
    rank = down_factor.shape[0]
    width_kv = up_factor.shape[0]
    own_rows = rank // n_data
    block = width_kv // (n_data * n_tensor)
    down16 = down_factor.astype(jnp.bfloat16)
    up16 = up_factor.astype(jnp.bfloat16)
    partial_in = jnp.dot(learn_acts, down16.T, preferred_element_type=jnp.float32)
    low_in = lax.psum(partial_in.astype(jnp.bfloat16), "tensor")
    low_out = jnp.dot(cotangent, up16, preferred_element_type=jnp.float32).astype(jnp.bfloat16)
    grad_acts = (
        jnp.dot(cotangent, base_weight.T, preferred_element_type=jnp.float32)
        + jnp.dot(low_out, down16, preferred_element_type=jnp.float32)
    ).astype(jnp.bfloat16)
    term_down = jnp.dot(low_out.T, learn_acts, preferred_element_type=jnp.float32)
    term_up = jnp.dot(cotangent.T, low_in, preferred_element_type=jnp.float32)
    owned_down, owned_up = (
        lax.psum_scatter(term_down, "dp", scatter_dimension=0, tiled=True),
        lax.psum_scatter(term_up, "dp", scatter_dimension=0, tiled=True),
    )
    span = width_kv // n_data
    old_down = lax.dynamic_slice_in_dim(down_factor, data_index * own_rows, own_rows, 0)
    old_up = lax.dynamic_slice_in_dim(up_factor, data_index * span, span, 0)
    new_down = update(old_down, owned_down, rate_down, total)
    rows_up = update(old_up, owned_up, rate_up, total)
    full_down, full_up = (
        lax.all_gather(new_down, "dp", axis=0, tiled=True),
        lax.all_gather(rows_up, "dp", axis=0, tiled=True),
    )
    new_up = lax.dynamic_slice_in_dim(rows_up, tensor_index * block, block, 0)
    merged = (
        base_weight.astype(jnp.float32)
        + jnp.dot(full_down.T, full_up.T, precision=lax.Precision.HIGHEST)
    ).astype(jnp.bfloat16)
    partial_out = jnp.dot(decode_acts, merged, preferred_element_type=jnp.float32)
    decoded = lax.psum(partial_out.astype(jnp.bfloat16), "tensor")
    return (grad_acts, new_down, new_up, decoded)


def solution(mesh):
    in_specs = (
        P("dp", "tensor"),
        P("dp", None),
        P("tensor", None),
        P(None, "tensor"),
        P(),
        P("dp", "tensor"),
    )
    out_specs = (P("dp", "tensor"), P("dp", "tensor"), P(("dp", "tensor"), None), P("dp", None))
    return jax.shard_map(body, mesh=mesh, in_specs=in_specs, out_specs=out_specs, check_vma=False)
```

profile of v0, /device:TPU:1, one launch (start us, length us, event | category | flops | bytes accessed | tf_op | source)
XLA Modules:
  0.0 774.1 jit_solution(14634783716885236617)
XLA Ops:
  7.2 0.0 copy-start
  7.2 0.0 copy-start.1
  7.2 0.0 copy-start.4
  7.2 0.0 all-reduce.5.cloned.1.call-start
  7.2 2.1 convolution_convert_fusion.1
  9.4 0.0 all-reduce.5.cloned.1.call-update
  9.4 0.0 all-reduce.9.cloned.1.call-start
  9.5 0.0 copy-done
  9.5 0.0 copy-done.4
  9.5 0.4 convolution_convert_fusion.2
  9.9 0.0 copy-done.1
  9.9 0.9 fusion.7
  10.8 0.0 all-reduce.9.cloned.1.call-update
  10.8 0.0 copy-start.3
  10.8 0.0 reduce-scatter.4.cloned.1.call-start
  10.9 157.7 %all-reduce.5.cloned.1.call-done = bf16[512,64]{1,0:T(8,128)(2,1)} async-done(((bf16[512,64]{1,0:T(8,128)(2,1)}), bf16[512,64]{1,0:T(8,128)(2,1)}) %all-reduce.5.cloned.1.call-update) | async-done | bytes 65552 | tf_op jit(solution)/shard_map/psum | solution.py:28
  168.6 1.2 convolution_bitcast_fusion
  169.8 1.0 copy.15
  170.8 0.0 copy-start.2
  170.8 0.0 reduce-scatter.4.cloned.1.call-update
  170.8 0.0 all-reduce.7.cloned.1.call-start
  170.9 1.3 dynamic-slice
  172.9 222.1 %all-reduce.9.cloned.1.call-done = f32[64,512]{1,0:T(8,128)} async-done(((f32[64,512]{1,0:T(8,128)}), f32[64,512]{1,0:T(8,128)}) %all-reduce.9.cloned.1.call-update) | async-done | bytes 131088
  395.0 0.0 copy-done.3
  395.0 0.7 fusion.5
  395.7 0.0 copy-start.5
  395.7 46.7 %all-gather = f32[32,2,512]{2,1,0:T(2,128)S(1)} all-gather(f32[1,2,512]{2,1,0:T(2,128)S(1)} %bitcast.20), channel_id=1, replica_groups=mesh['dp'=32,'tensor'=16] {'dp'}, dimensions={0}, use_global_device_ids=true | all-gather | bytes 135168 | tf_op jit(solution)/shard_map/all_gather | solution.py:46
  442.5 0.1 reshape.9
  442.6 83.3 %reduce-scatter.4.cloned.1.call-done = f32[32,64]{1,0:T(8,128)} async-done(((f32[1024,64]{1,0:T(8,128)}), f32[32,64]{1,0:T(8,128)}) %reduce-scatter.4.cloned.1.call-update) | async-done | bytes 8208
  525.9 0.8 copy.16
  526.7 0.1 multiply_subtract_fusion
  526.8 0.1 copy.12
  526.9 49.1 %all_gather.7 = f32[1024,64]{1,0:T(8,128)S(1)} all-gather(f32[32,64]{1,0:T(8,128)S(1)} %copy.12), channel_id=1, replica_groups=mesh['dp'=32,'tensor'=16] {'dp'}, dimensions={0}, use_global_device_ids=true | all-gather | bytes 270336 | tf_op jit(solution)/shard_map/all_gather | solution.py:47
  576.0 0.0 copy-done.2
  576.0 0.0 copy-start.6
  576.0 1.9 add_convert_fusion
  577.9 0.0 copy-done.5
  577.9 0.0 copy-done.6
  577.9 1.7 fusion
  579.6 0.0 all-reduce.7.cloned.1.call-update
  579.6 0.7 fusion.6
  580.4 1.1 fusion.1
  581.5 0.1 constant_dynamic-slice_fusion
  581.6 0.6 copy.13
  582.2 183.0 %all-reduce.7.cloned.1.call-done = bf16[512,1024]{0,1:T(8,128)(2,1)} async-done(((bf16[512,1024]{0,1:T(8,128)(2,1)}), bf16[512,1024]{0,1:T(8,128)(2,1)}) %all-reduce.7.cloned.1.call-update) | async-done | bytes 1048592 | tf_op jit(solution)/shard_map/psum | solution.py:55
  765.3 2.3 copy.14
Async XLA Ops:
  7.2 2.3 copy-start
  7.2 2.7 copy-start.1
  7.2 2.3 copy-start.4
  7.2 161.4 %all-reduce.5.cloned.1.call-start = ((), (), s32[]{:S(2)}) async-start(), calls=%async_computation.1 | async-start | bytes 262144 | tf_op jit(solution)/shard_map/psum | solution.py:28
  9.4 385.6 %all-reduce.9.cloned.1.call-start = ((), (), s32[]{:S(2)}) async-start(), calls=%async_computation.4 | async-start | bytes 262144
  10.8 384.2 %copy-start.3 = (f32[64,512]{1,0:T(8,128)S(1)}, f32[64,512]{1,0:T(8,128)}, u32[]{:S(2)}) copy-start(f32[64,512]{1,0:T(8,128)} %param.9) | copy-start | bytes 393220
  10.8 515.1 %reduce-scatter.4.cloned.1.call-start = ((), (), s32[]{:S(2)}) async-start(), calls=%async_computation.3 | async-start | bytes 540672
  170.8 405.1 %copy-start.2 = (bf16[512,1024]{1,0:T(8,128)(2,1)S(1)}, bf16[512,1024]{1,0:T(8,128)(2,1)}, u32[]{:S(2)}) copy-start(bf16[512,1024]{1,0:T(8,128)(2,1)} %param.8) | copy-start | bytes 3145732
  170.8 594.4 %all-reduce.7.cloned.1.call-start = ((), (), s32[]{:S(2)}) async-start(), calls=%async_computation.2 | async-start | bytes 2097152 | tf_op jit(solution)/shard_map/psum | solution.py:55
  395.7 182.1 %copy-start.5 = (f32[2,512]{1,0:T(2,128)}, f32[2,512]{1,0:T(2,128)S(1)}, u32[]{:S(2)}) copy-start(f32[2,512]{1,0:T(2,128)S(1)} %fusion.5) | copy-start | bytes 12292
  576.0 1.9 copy-start.6
Sparse Core Ops, SparseCore 0:
  11.5 157.0 all-reduce.4
  172.3 222.6 all-reduce.8
  398.4 127.4 reduce-scatter.3
  579.8 185.4 all-reduce.6
where the time goes:
time: 774 us
  waiting for transfers between devices  646 us (83%)
  blocking collectives  95.8 us (12%)
  between operations  14.5 us (2%)
  matrix products  10.1 us (1%)
    unnamed x6, waiting for transfers between devices  306 us
    psum x1, waiting for transfers between devices, body(): decoded = lax.psum(partial_out.astype(jnp.bfloat16), 'tensor')  183 us
    psum x1, waiting for transfers between devices, body(): low_in = lax.psum(partial_in.astype(jnp.bfloat16), 'tensor')  158 us
    all_gather x1, blocking collectives, body(): lax.all_gather(rows_up, 'dp', axis=0, tiled=True)  49.1 us
    all_gather x1, blocking collectives, body(): lax.all_gather(new_down, 'dp', axis=0, tiled=True)  46.7 us
  transfers between devices with their start and end apart: 4, of which 4 were waited for; matrix products, arithmetic and copies ran while one was open for 1% of the time, Pallas kernels for 0%

commit v1 on v0

v1 whole, which is shorter than its diff:
```python
import jax
import jax.numpy as jnp
from jax import lax
from jax.experimental import pallas as pl
from jax.experimental.pallas import tpu as pltpu
from jax.sharding import PartitionSpec as P

rate_down = 0.2
rate_up = 3.0

NZ = 16
GZ = 4
NA = 8
NB = 4
NC = 8

BF = jnp.bfloat16
F32 = jnp.float32

(D_A, D_B, D_C, U_PAIR, U_RS, U_A, U_B, U_AG, U_PAIR2,
 M_PAIR, M_RS, M_AG, M_PAIR2, L_PAIR, L_ALL, L_PAIR2) = range(16)
(I_COT, I_UP, I_LEARN, I_DOWN, I_DEC, I_BASE,
 O_GA, O_ND, O_NU, O_NUT, O_LD, O_M) = range(12)


def dot(a, b, ca, cb):
    return lax.dot_general(a, b, (((ca,), (cb,)), ((), ())), preferred_element_type=F32)


def comm_kernel(
    learn_h, cot_h, base_h, down_h, up_h, dec_h,
    ga_h, nd_h, nu_h, nut_h, ld_h, m_h,
    learn, cot, base, down, up, dec, ga,
    lowout, td_send, d_a, d_b, d_c, ndown, nd_out,
    g32, u_send, u_prec, u_sum, u_rs, u_a, u_b, u_fin, upt, nupt16, nup, nu_out,
    m_send, m_keep, m_prec, m_sum, m_rs, m_fin,
    l32, l_send, l_prec, l_all, l_fin,
    ssem, rsem, lsem,
):
    d = lax.axis_index("dp")
    t = lax.axis_index("tensor")
    x = d // NZ
    z = d % NZ
    zb = z // GZ
    za = z % GZ
    a = x * GZ + za
    q = t // 2
    c = t % 2
    oc = 1 - c
    total = 16384.0

    def load(src, dst, i):
        cp = pltpu.make_async_copy(src, dst, lsem.at[i])
        cp.start()
        return cp

    cp_cot = load(cot_h, cot, I_COT)
    cp_up = load(up_h, up, I_UP)
    cp_learn = load(learn_h, learn, I_LEARN)
    cp_down = load(down_h, down, I_DOWN)
    cp_dec = load(dec_h, dec, I_DEC)
    cp_base = load(base_h, base, I_BASE)

    def near(k):
        other = (a + k) % NA
        return other, {"dp": (other // GZ) * NZ + zb * GZ + other % GZ, "tensor": t}

    def far(k):
        return {"dp": x * NZ + ((zb + k) % NB) * GZ + za, "tensor": t}

    def chip(k):
        other = (q + k) % NC
        return other, {"dp": d, "tensor": other * 2 + c}

    pair = {"dp": d, "tensor": q * 2 + oc}

    barrier = pltpu.get_barrier_semaphore()

    def greet(dev):
        pl.semaphore_signal(barrier, inc=1, device_id=dev, device_id_type=pl.DeviceIdType.MESH)

    def hello_near(k, _):
        greet(near(k)[1])
        return 0

    def hello_far(k, _):
        greet(far(k))
        return 0

    def hello_chip(k, _):
        greet(chip(k)[1])
        return 0

    lax.fori_loop(1, NB, hello_far, 0)
    lax.fori_loop(1, NA, hello_near, 0)
    lax.fori_loop(1, NC, hello_chip, 0)
    greet(pair)

    def remote(src, dst, i, dev):
        return pltpu.make_async_remote_copy(
            src_ref=src, dst_ref=dst, send_sem=ssem.at[i], recv_sem=rsem.at[i],
            device_id=dev, device_id_type=pl.DeviceIdType.MESH,
        )

    def arrived(ref, i):
        remote(ref, ref, i, pair).wait_recv()

    def sent(ref, i):
        remote(ref, ref, i, pair).wait_send()

    def to_near(i, src, dst):
        def step(k, _):
            other, dev = near(k)
            remote(src(other), dst, i, dev).start()
            return 0
        lax.fori_loop(1, NA, step, 0)

    def to_far(i, src, dst):
        def step(k, _):
            remote(src, dst, i, far(k)).start()
            return 0
        lax.fori_loop(1, NB, step, 0)

    def to_chips(i, src, dst):
        def step(k, _):
            other, dev = chip(k)
            remote(src(other), dst, i, dev).start()
            return 0
        lax.fori_loop(1, NC, step, 0)

    def total_of(ref):
        acc = ref[0].astype(F32)
        for k in range(1, ref.shape[0]):
            acc = acc + ref[k].astype(F32)
        return acc

    def two_rows(ref, block, first):
        rows = ref[pl.ds(pl.multiple_of(block * 8, 8), 8), :]
        at = lax.broadcasted_iota(jnp.int32, rows.shape, 0)
        picked = [
            jnp.sum(jnp.where(at == first + k, rows, 0.0), axis=0, keepdims=True) for k in range(2)
        ]
        return jnp.concatenate(picked, axis=0)

    cp_cot.wait()
    cp_up.wait()
    lowout[...] = dot(cot[...], up[...].astype(BF), 1, 0).astype(BF)
    cp_learn.wait()
    term = dot(lowout[...], learn[...], 0, 0).astype(BF)
    for k in range(NA):
        i, j = k // 4, k % 4
        td_send[k] = term[32 * i:32 * i + 32, 128 * j:128 * j + 128]
    d_a[a] = td_send[a]

    pl.semaphore_wait(barrier, (NB - 1) + (NA - 1) + (NC - 1) + 1)
    to_near(D_A, lambda o: td_send.at[o], d_a.at[a])

    cp_down.wait()
    down16 = down[...].astype(BF)
    low_in = dot(down16, learn[...], 1, 1).astype(BF)
    term_up = dot(low_in, cot[...], 1, 0)
    for i in range(2):
        for j in range(NC):
            g32[i, j] = term_up[32 * i:32 * i + 32, 128 * j:128 * j + 128]
    u_send[...] = g32[oc].astype(BF)
    remote(u_send, u_prec, U_PAIR, pair).start()

    cp_dec.wait()
    cp_base.wait()

    def other_half(r, _):
        rows = pl.ds(pl.multiple_of(r * 128, 128), 128)
        cols = pl.ds(pl.multiple_of(oc * 512, 512), 512)
        m_send[rows, :] = dot(dec[rows, :], base[:, cols], 1, 0).astype(BF)
        return 0

    def own_half(r, _):
        rows = pl.ds(pl.multiple_of(r * 128, 128), 128)
        cols = pl.ds(pl.multiple_of(c * 512, 512), 512)
        m_keep[rows, :] = dot(dec[rows, :], base[:, cols], 1, 0)
        return 0

    lax.fori_loop(0, 4, other_half, 0)
    remote(m_send, m_prec, M_PAIR, pair).start()

    arrived(u_prec, U_PAIR)
    u_sum[...] = (g32[c] + u_prec[...].astype(F32)).astype(BF)
    u_rs[q] = u_sum[q]
    to_chips(U_RS, lambda o: u_sum.at[o], u_rs.at[q])

    lax.fori_loop(0, 4, own_half, 0)
    arrived(m_prec, M_PAIR)

    def add_half(r, _):
        rows = pl.ds(pl.multiple_of(r * 64, 64), 64)
        m_sum[r] = (m_keep[rows, :] + m_prec[rows, :].astype(F32)).astype(BF)
        return 0

    lax.fori_loop(0, NC, add_half, 0)
    m_rs[q] = m_sum[q]

    arrived(d_a.at[pl.ds(0, NA - 1)], D_A)
    d_b[zb] = total_of(d_a).astype(BF)
    to_far(D_B, d_b.at[zb], d_b.at[zb])

    to_chips(M_RS, lambda o: m_sum.at[o], m_rs.at[q])

    def acts(r, _):
        rows = pl.ds(pl.multiple_of(r * 128, 128), 128)
        ga[rows, :] = (
            dot(cot[rows, :], base[...], 1, 1) + dot(lowout[rows, :], down[...].astype(BF), 1, 0)
        ).astype(BF)
        return 0

    lax.fori_loop(0, 4, acts, 0)
    cp_ga = load(ga, ga_h, O_GA)
    upt[...] = up[...].T

    arrived(u_rs.at[pl.ds(0, NC - 1)], U_RS)
    u_a[a] = total_of(u_rs).astype(BF)
    to_near(U_A, lambda o: u_a.at[a], u_a.at[a])

    arrived(u_a.at[pl.ds(0, NA - 1)], U_A)
    u_b[zb] = total_of(u_a).astype(BF)
    to_far(U_B, u_b.at[zb], u_b.at[zb])

    arrived(d_b.at[pl.ds(0, NB - 1)], D_B)
    d_c[a] = total_of(d_b).astype(BF)
    to_near(D_C, lambda o: d_c.at[a], d_c.at[a])

    my_rows = pl.ds(pl.multiple_of(q * 64, 64), 64)
    arrived(m_rs.at[pl.ds(0, NC - 1)], M_RS)
    m_fin[c, my_rows, :] = total_of(m_rs).astype(BF)
    to_chips(M_AG, lambda o: m_fin.at[c, my_rows], m_fin.at[c, my_rows])

    arrived(d_c.at[pl.ds(0, NA - 1)], D_C)
    for k in range(NA):
        i, j = k // 4, k % 4
        rows, cols = pl.ds(32 * i, 32), pl.ds(128 * j, 128)
        grad = d_c[k].astype(F32) / total
        ndown[rows, cols] = down[rows, cols] - rate_down * grad
    l32[...] = dot(ndown[...].astype(BF), dec[...], 1, 1)
    l_send[...] = l32[pl.ds(pl.multiple_of(oc * 32, 32), 32), :].astype(BF)
    remote(l_send, l_prec, L_PAIR, pair).start()
    nd_out[...] = two_rows(ndown, d // 4, 2 * (d % 4))
    cp_nd = load(nd_out, nd_h, O_ND)
    arrived(l_prec, L_PAIR)
    l_all[q] = (l32[pl.ds(pl.multiple_of(c * 32, 32), 32), :] + l_prec[...].astype(F32)).astype(BF)
    to_chips(L_ALL, lambda o: l_all.at[q], l_all.at[q])

    arrived(u_b.at[pl.ds(0, NB - 1)], U_B)
    u_fin[c, q] = total_of(u_b).astype(BF)
    to_chips(U_AG, lambda o: u_fin.at[c, q], u_fin.at[c, q])

    arrived(m_fin.at[c, pl.ds(0, 448)], M_AG)
    remote(m_fin.at[c], m_fin.at[c], M_PAIR2, pair).start()

    arrived(u_fin.at[c, pl.ds(0, NC - 1)], U_AG)
    remote(u_fin.at[c], u_fin.at[c], U_PAIR2, pair).start()

    arrived(m_fin.at[oc], M_PAIR2)
    cp_m = load(m_fin, m_h, O_M)

    arrived(u_fin.at[oc], U_PAIR2)
    for i in range(2):
        for j in range(NC):
            rows, cols = pl.ds(32 * i, 32), pl.ds(128 * j, 128)
            grad = u_fin[i, j].astype(F32) / total
            upt[rows, cols] = upt[rows, cols] - rate_up * grad
    nupt16[...] = upt[...].astype(BF)
    cp_nut = load(nupt16, nut_h, O_NUT)
    nup[...] = upt[...].T
    nu_out[...] = two_rows(nup, d * 4 + t // 4, 2 * (t % 4))
    cp_nu = load(nu_out, nu_h, O_NU)

    half = pl.ds(pl.multiple_of(c * 32, 32), 32)
    arrived(l_all.at[pl.ds(0, NC - 1)], L_ALL)
    l_fin[half, :] = total_of(l_all).astype(BF)
    remote(l_fin.at[half], l_fin.at[half], L_PAIR2, pair).start()
    arrived(l_fin.at[half], L_PAIR2)
    cp_ld = load(l_fin, ld_h, O_LD)

    m_part = m_fin.at[c, pl.ds(0, 448)]
    for ref, i in (
        (td_send.at[pl.ds(0, NA - 1)], D_A), (d_b.at[pl.ds(0, NB - 1)], D_B),
        (d_c.at[pl.ds(0, NA - 1)], D_C), (u_send, U_PAIR), (u_rs.at[pl.ds(0, NC - 1)], U_RS),
        (u_a.at[pl.ds(0, NA - 1)], U_A), (u_b.at[pl.ds(0, NB - 1)], U_B),
        (u_fin.at[c, pl.ds(0, NC - 1)], U_AG), (u_fin.at[c], U_PAIR2), (m_send, M_PAIR),
        (m_rs.at[pl.ds(0, NC - 1)], M_RS), (m_part, M_AG), (m_fin.at[c], M_PAIR2),
        (l_send, L_PAIR), (l_all.at[pl.ds(0, NC - 1)], L_ALL), (l_fin.at[half], L_PAIR2),
    ):
        sent(ref, i)
    for cp in (cp_ga, cp_nd, cp_m, cp_nut, cp_nu, cp_ld):
        cp.wait()


def finish_kernel(m_ref, ld_ref, nut_ref, ga_in, nd_in, nu_in, dec_out, ga_out, nd_out, nu_out, sem):
    step = pl.program_id(0)

    def copies():
        return [
            pltpu.make_async_copy(s, o, sem.at[i])
            for i, (s, o) in enumerate(((ga_in, ga_out), (nd_in, nd_out), (nu_in, nu_out)))
        ]

    @pl.when(step == 0)
    def _():
        for cp in copies():
            cp.start()

    corr = dot(ld_ref[...], nut_ref[...], 0, 0)
    for h in range(2):
        cols = slice(512 * h, 512 * h + 512)
        dec_out[:, cols] = (m_ref[h].astype(F32) + corr[:, cols]).astype(BF)

    @pl.when(step == pl.num_programs(0) - 1)
    def _():
        for cp in copies():
            cp.wait()


def body(learn_acts, cotangent, base_weight, down_factor, up_factor, decode_acts):
    any_ = pl.BlockSpec(memory_space=pl.ANY)
    V = pltpu.VMEM
    sds = jax.ShapeDtypeStruct
    ga, nd, nu, nut, ld, m = pl.pallas_call(
        comm_kernel,
        out_shape=(
            sds((512, 512), BF), sds((2, 512), F32), sds((2, 64), F32),
            sds((64, 1024), BF), sds((64, 512), BF), sds((2, 512, 512), BF),
        ),
        in_specs=[any_] * 6,
        out_specs=(any_,) * 6,
        scratch_shapes=[
            V((512, 512), BF), V((512, 1024), BF), V((512, 1024), BF), V((64, 512), F32),
            V((1024, 64), F32), V((512, 512), BF), V((512, 512), BF),
            V((512, 64), BF), V((NA, 32, 128), BF), V((NA, 32, 128), BF), V((NB, 32, 128), BF),
            V((NA, 32, 128), BF), V((64, 512), F32), V((2, 512), F32),
            V((2, NC, 32, 128), F32), V((NC, 32, 128), BF), V((NC, 32, 128), BF),
            V((NC, 32, 128), BF), V((NC, 32, 128), BF), V((NA, 32, 128), BF), V((NB, 32, 128), BF),
            V((2, NC, 32, 128), BF), V((64, 1024), F32), V((64, 1024), BF), V((1024, 64), F32),
            V((2, 64), F32),
            V((512, 512), BF), V((512, 512), F32), V((512, 512), BF), V((NC, 64, 512), BF),
            V((NC, 64, 512), BF), V((2, 512, 512), BF),
            V((64, 512), F32), V((32, 512), BF), V((32, 512), BF), V((NC, 32, 512), BF),
            V((64, 512), BF),
            pltpu.SemaphoreType.DMA((16,)), pltpu.SemaphoreType.DMA((16,)),
            pltpu.SemaphoreType.DMA((12,)),
        ],
        compiler_params=pltpu.CompilerParams(
            collective_id=0, has_side_effects=True, vmem_limit_bytes=48 * 1024 * 1024
        ),
        name="adapter_step",
    )(learn_acts, cotangent, base_weight, down_factor, up_factor, decode_acts)
    tile = 128
    decoded, ga, nd, nu = pl.pallas_call(
        finish_kernel,
        grid=(512 // tile,),
        out_shape=(
            sds((512, 1024), BF), sds((512, 512), BF), sds((2, 512), F32), sds((2, 64), F32),
        ),
        in_specs=[
            pl.BlockSpec((2, tile, 512), lambda i: (0, i, 0)),
            pl.BlockSpec((64, tile), lambda i: (0, i)),
            pl.BlockSpec((64, 1024), lambda i: (0, 0)),
            any_, any_, any_,
        ],
        out_specs=(pl.BlockSpec((tile, 1024), lambda i: (i, 0)), any_, any_, any_),
        scratch_shapes=[pltpu.SemaphoreType.DMA((3,))],
        name="finish",
    )(m, ld, nut, ga, nd, nu)
    return (ga, nd, nu, decoded)


def solution(mesh):
    in_specs = (
        P("dp", "tensor"),
        P("dp", None),
        P("tensor", None),
        P(None, "tensor"),
        P(),
        P("dp", "tensor"),
    )
    out_specs = (P("dp", "tensor"), P("dp", "tensor"), P(("dp", "tensor"), None), P("dp", None))
    return jax.shard_map(body, mesh=mesh, in_specs=in_specs, out_specs=out_specs, check_vma=False)
```

time: 774 us -> 75.2 us (0.10)
  waiting for transfers between devices: 646 us -> 0 us
  blocking collectives: 95.8 us -> 0 us
  Pallas kernels: 0 us -> 65.3 us
  between operations: 14.5 us -> 0.7 us
  matrix products: 10.1 us -> 0 us
    psum x2 -> x0, waiting for transfers between devices: 341 us -> none  [the longest x1 183 us: body(): decoded = lax.psum(partial_out.astype(jnp.bfloat16), 'tensor')]
    unnamed x6 -> x0, waiting for transfers between devices: 306 us -> none
    all_gather x2 -> x0, blocking collectives: 95.8 us -> none  [the longest x1 49.1 us: body(): lax.all_gather(rows_up, 'dp', axis=0, tiled=True)]
    pallas_call x0 -> x2, Pallas kernels: none -> 65.3 us  [the longest x1 46.5 us: body(): pl.pallas_call(comm_kernel, out_shape=(sds((512, 512), BF), sds((2, 512),...]
    dot_general x8 -> x0, matrix products: 10.1 us -> none  [the longest x1 2.14 us: body(): jnp.dot(learn_acts, down16.T, preferred_element_type=jnp.float32)]
  transfers between devices with their start and end apart: 4 -> 0, of which waited for: 4 -> 0; matrix products, arithmetic and copies ran while one was open for 1% -> 0% of each run, Pallas kernels for 0% -> 0%
where the time goes in v1:
time: 75.2 us; the launch traced here: 74.9 us
  Pallas kernels  65.3 us (87%)
  local copies, waits for them, and re-layouts  8.88 us (12%)
    pallas_call x1, Pallas kernels, body(): pl.pallas_call(comm_kernel, out_shape=(sds((512, 512), BF), sds((2, 512),...  46.5 us
    pallas_call x1, Pallas kernels, body(): pl.pallas_call(finish_kernel, grid=(512 // tile,), out_shape=(sds((512, 1...  18.9 us
    unnamed x23, local copies, waits for them, and re-layouts  8.88 us

profile of v1, /device:TPU:1, one launch (start us, length us, event | category | flops | bytes accessed | tf_op | source)
XLA Modules:
  0.0 74.9 jit_solution(8562471444630777901)
XLA Ops:
  0.6 0.0 copy-start.7
  0.6 0.0 copy-start.4
  0.7 1.2 %copy.10.up_h = f32[1024,64]{1,0:T(8,128)S(1)} copy(f32[1024,64]{0,1:T(8,128)} %param.10) | data formatting | bytes 524288 | tf_op args[4]
  1.9 0.0 copy-done.7
  1.9 0.0 copy-done.4
  1.9 0.0 copy-start.1
  1.9 1.2 %copy-done.1 = bf16[512,1024]{1,0:T(8,128)(2,1)S(1)} copy-done((bf16[512,1024]{1,0:T(8,128)(2,1)S(1)}, bf16[512,1024]{1,0:T(8,128)(2,1)}, u32[]{:S(2)}) %copy-start.1) | copy-done | bytes 1048600
  3.1 0.0 copy-start.2
  3.1 1.2 %copy-done.2 = bf16[512,1024]{1,0:T(8,128)(2,1)S(1)} copy-done((bf16[512,1024]{1,0:T(8,128)(2,1)S(1)}, bf16[512,1024]{1,0:T(8,128)(2,1)}, u32[]{:S(2)}) %copy-start.2) | copy-done | bytes 1048600
  4.3 0.0 copy-start.5
  4.3 1.0 %copy-done.5 = bf16[512,512]{1,0:T(8,128)(2,1)S(1)} copy-done((bf16[512,512]{1,0:T(8,128)(2,1)S(1)}, bf16[512,512]{1,0:T(8,128)(2,1)}, u32[]{:S(2)}) %copy-start.5) | copy-done | bytes 524312
  5.4 46.5 %adapter_step.1 = (bf16[512,512]{1,0:T(8,128)(2,1)S(1)}, f32[2,512]{1,0:T(2,128)S(1)}, f32[2,64]{1,0:T(2,128)S(1)}, bf16[64,1024]{1,0:T(8,128)(2,1)S(1)}, bf16[6...) custom-call(bf16[512,512]{1,0:T(8,128)(2,1)S(1)} %copy-done.4, bf16[512,1024]{1,0:T(8,128)(2,1)S(1)} %copy-done.1, ...), custom_call_target="tpu_custom_call" | custom-call | tf_op jit(solution)/shard_map/adapter_step/pallas_call | solution.py:326
  51.8 0.0 copy-start
  51.9 1.0 %copy-done = bf16[2,512,512]{2,1,0:T(8,128)(2,1)} copy-done((bf16[2,512,512]{2,1,0:T(8,128)(2,1)}, bf16[2,512,512]{2,1,0:T(8,128)(2,1)S(1)}, u32[]{:S(2)}) %copy-start) | copy-done | bytes 1048600
  52.8 0.0 copy-start.3
  52.8 0.8 %copy-done.3 = bf16[512,512]{1,0:T(8,128)(2,1)} copy-done((bf16[512,512]{1,0:T(8,128)(2,1)}, bf16[512,512]{1,0:T(8,128)(2,1)S(1)}, u32[]{:S(2)}) %copy-start.3) | copy-done | bytes 524312
  53.6 0.0 copy-start.6
  53.6 0.6 copy-done.6
  54.3 0.0 copy-start.8
  54.3 0.6 copy-done.8
  54.9 0.0 copy-start.10
  54.9 0.5 copy-done.10
  55.4 0.0 copy-start.9
  55.5 0.6 copy-done.9
  56.0 18.9 %finish.1 = (bf16[512,1024]{1,0:T(8,128)(2,1)}, bf16[512,512]{1,0:T(8,128)(2,1)}, f32[2,512]{1,0:T(2,128)}, f32[2,64]{1,0:T(2,128)}) custom-call(bf16[2,512,512]{2,1,0:T(8,128)(2,1)} %copy-done, bf16[64,512]{1,0:T(8,128)(2,1)} %copy-done.8, bf16[64,1024]{1,0:T(8,128)(2,1)} %copy-done.6, bf16[512,512]{1,0:T(8,128)(2,1)} %copy-done.3, f32[2,512]{1,0:T(2,128)} %copy-done.9, ...), custom_call_target="tpu_custom_call" | custom-call | tf_op jit(solution)/shard_map/finish/pallas_call | solution.py:356
Async XLA Ops:
  0.6 1.2 %copy-start.7 = (f32[64,512]{1,0:T(8,128)S(1)}, f32[64,512]{1,0:T(8,128)}, u32[]{:S(2)}) copy-start(f32[64,512]{1,0:T(8,128)} %down_h.1) | copy-start | bytes 393220
  0.6 1.2 %copy-start.4 = (bf16[512,512]{1,0:T(8,128)(2,1)S(1)}, bf16[512,512]{1,0:T(8,128)(2,1)}, u32[]{:S(2)}) copy-start(bf16[512,512]{1,0:T(8,128)(2,1)} %learn_h.1) | copy-start | bytes 1572868
  1.9 1.2 %copy-start.1 = (bf16[512,1024]{1,0:T(8,128)(2,1)S(1)}, bf16[512,1024]{1,0:T(8,128)(2,1)}, u32[]{:S(2)}) copy-start(bf16[512,1024]{1,0:T(8,128)(2,1)} %cot_h.1) | copy-start | bytes 3145732
  3.1 1.2 %copy-start.2 = (bf16[512,1024]{1,0:T(8,128)(2,1)S(1)}, bf16[512,1024]{1,0:T(8,128)(2,1)}, u32[]{:S(2)}) copy-start(bf16[512,1024]{1,0:T(8,128)(2,1)} %base_h.1) | copy-start | bytes 3145732
  4.3 1.0 %copy-start.5 = (bf16[512,512]{1,0:T(8,128)(2,1)S(1)}, bf16[512,512]{1,0:T(8,128)(2,1)}, u32[]{:S(2)}) copy-start(bf16[512,512]{1,0:T(8,128)(2,1)} %dec_h.1) | copy-start | bytes 1572868
  51.8 1.0 %copy-start = (bf16[2,512,512]{2,1,0:T(8,128)(2,1)}, bf16[2,512,512]{2,1,0:T(8,128)(2,1)S(1)}, u32[]{:S(2)}) copy-start(bf16[2,512,512]{2,1,0:T(8,128)(2,1)S(1)} %get-tuple-element.14.m_ref) | copy-start | bytes 3145732
  52.8 0.8 %copy-start.3 = (bf16[512,512]{1,0:T(8,128)(2,1)}, bf16[512,512]{1,0:T(8,128)(2,1)S(1)}, u32[]{:S(2)}) copy-start(bf16[512,512]{1,0:T(8,128)(2,1)S(1)} %get-tuple-element.17.ga_in) | copy-start | bytes 1572868
  53.6 0.6 copy-start.6
  54.3 0.6 copy-start.8
  54.9 0.5 copy-start.10
  55.4 0.6 copy-start.9

commit v2 on v1

--- a/solution.py
+++ b/solution.py
@@ -30,7 +30,7 @@
 def comm_kernel(
     learn_h, cot_h, base_h, down_h, up_h, dec_h,
     ga_h, nd_h, nu_h, nut_h, ld_h, m_h,
-    learn, cot, base, down, up, dec, ga,
+    learn, cot, base, down, dec, ga,
     lowout, td_send, d_a, d_b, d_c, ndown, nd_out,
     g32, u_send, u_prec, u_sum, u_rs, u_a, u_b, u_fin, upt, nupt16, nup, nu_out,
     m_send, m_keep, m_prec, m_sum, m_rs, m_fin,
@@ -55,7 +55,7 @@
         return cp
 
     cp_cot = load(cot_h, cot, I_COT)
-    cp_up = load(up_h, up, I_UP)
+    cp_up = load(up_h, upt, I_UP)
     cp_learn = load(learn_h, learn, I_LEARN)
     cp_down = load(down_h, down, I_DOWN)
     cp_dec = load(dec_h, dec, I_DEC)
@@ -144,7 +144,7 @@
 
     cp_cot.wait()
     cp_up.wait()
-    lowout[...] = dot(cot[...], up[...].astype(BF), 1, 0).astype(BF)
+    lowout[...] = dot(cot[...], upt[...].astype(BF), 1, 1).astype(BF)
     cp_learn.wait()
     term = dot(lowout[...], learn[...], 0, 0).astype(BF)
     for k in range(NA):
@@ -214,7 +214,6 @@
 
     lax.fori_loop(0, 4, acts, 0)
     cp_ga = load(ga, ga_h, O_GA)
-    upt[...] = up[...].T
 
     arrived(u_rs.at[pl.ds(0, NC - 1)], U_RS)
     u_a[a] = total_of(u_rs).astype(BF)
@@ -294,33 +293,31 @@
         cp.wait()
 
 
-def finish_kernel(m_ref, ld_ref, nut_ref, ga_in, nd_in, nu_in, dec_out, ga_out, nd_out, nu_out, sem):
-    step = pl.program_id(0)
-
-    def copies():
-        return [
-            pltpu.make_async_copy(s, o, sem.at[i])
-            for i, (s, o) in enumerate(((ga_in, ga_out), (nd_in, nd_out), (nu_in, nu_out)))
-        ]
-
-    @pl.when(step == 0)
-    def _():
-        for cp in copies():
-            cp.start()
-
-    corr = dot(ld_ref[...], nut_ref[...], 0, 0)
-    for h in range(2):
-        cols = slice(512 * h, 512 * h + 512)
-        dec_out[:, cols] = (m_ref[h].astype(F32) + corr[:, cols]).astype(BF)
-
-    @pl.when(step == pl.num_programs(0) - 1)
-    def _():
-        for cp in copies():
-            cp.wait()
+def finish_kernel(m_ref, ld_ref, nut_ref, ga_ref, nd_ref, nu_ref, dec_h, ga_h, nd_h, nu_h, dec_v, sem):
+    small = [
+        pltpu.make_async_copy(ref, out, sem.at[4 + i])
+        for i, (ref, out) in enumerate(((ga_ref, ga_h), (nd_ref, nd_h), (nu_ref, nu_h)))
+    ]
+    for cp in small:
+        cp.start()
+    parts = []
+    for r in range(4):
+        rows = slice(128 * r, 128 * r + 128)
+        corr = dot(ld_ref[:, rows], nut_ref[...], 0, 0)
+        for h in range(2):
+            cols = slice(512 * h, 512 * h + 512)
+            dec_v[rows, cols] = (m_ref[h, rows, :].astype(F32) + corr[:, cols]).astype(BF)
+        cp = pltpu.make_async_copy(dec_v.at[rows], dec_h.at[rows], sem.at[r])
+        cp.start()
+        parts.append(cp)
+    for cp in parts + small:
+        cp.wait()
 
 
 def body(learn_acts, cotangent, base_weight, down_factor, up_factor, decode_acts):
     any_ = pl.BlockSpec(memory_space=pl.ANY)
+    hbm = pl.BlockSpec(memory_space=pltpu.HBM)
+    vmem = pl.BlockSpec(memory_space=pltpu.VMEM)
     V = pltpu.VMEM
     sds = jax.ShapeDtypeStruct
     ga, nd, nu, nut, ld, m = pl.pallas_call(
@@ -329,11 +326,11 @@
             sds((512, 512), BF), sds((2, 512), F32), sds((2, 64), F32),
             sds((64, 1024), BF), sds((64, 512), BF), sds((2, 512, 512), BF),
         ),
-        in_specs=[any_] * 6,
+        in_specs=[hbm] * 6,
         out_specs=(any_,) * 6,
         scratch_shapes=[
             V((512, 512), BF), V((512, 1024), BF), V((512, 1024), BF), V((64, 512), F32),
-            V((1024, 64), F32), V((512, 512), BF), V((512, 512), BF),
+            V((512, 512), BF), V((512, 512), BF),
             V((512, 64), BF), V((NA, 32, 128), BF), V((NA, 32, 128), BF), V((NB, 32, 128), BF),
             V((NA, 32, 128), BF), V((64, 512), F32), V((2, 512), F32),
             V((2, NC, 32, 128), F32), V((NC, 32, 128), BF), V((NC, 32, 128), BF),
@@ -351,22 +348,21 @@
             collective_id=0, has_side_effects=True, vmem_limit_bytes=48 * 1024 * 1024
         ),
         name="adapter_step",
-    )(learn_acts, cotangent, base_weight, down_factor, up_factor, decode_acts)
-    tile = 128
+    )(*(
+        pltpu.with_memory_space_constraint(arg, pltpu.HBM)
+        for arg in (
+            learn_acts, cotangent, base_weight, down_factor, up_factor.T, decode_acts
+        )
+    ))
     decoded, ga, nd, nu = pl.pallas_call(
         finish_kernel,
-        grid=(512 // tile,),
         out_shape=(
             sds((512, 1024), BF), sds((512, 512), BF), sds((2, 512), F32), sds((2, 64), F32),
         ),
-        in_specs=[
-            pl.BlockSpec((2, tile, 512), lambda i: (0, i, 0)),
-            pl.BlockSpec((64, tile), lambda i: (0, i)),
-            pl.BlockSpec((64, 1024), lambda i: (0, 0)),
-            any_, any_, any_,
-        ],
-        out_specs=(pl.BlockSpec((tile, 1024), lambda i: (i, 0)), any_, any_, any_),
-        scratch_shapes=[pltpu.SemaphoreType.DMA((3,))],
+        in_specs=[vmem] * 6,
+        out_specs=(hbm,) * 4,
+        scratch_shapes=[V((512, 1024), BF), pltpu.SemaphoreType.DMA((7,))],
+        compiler_params=pltpu.CompilerParams(vmem_limit_bytes=16 * 1024 * 1024),
         name="finish",
     )(m, ld, nut, ga, nd, nu)
     return (ga, nd, nu, decoded)

time: 75.2 us -> 48.1 us (0.64)
  Pallas kernels: 65.3 us -> 47.3 us
  local copies, waits for them, and re-layouts: 8.88 us -> 0 us
    pallas_call x1, Pallas kernels: 18.9 us -> 1.29 us  [body(): pl.pallas_call(finish_kernel, out_shape=(sds((512, 1024), BF), sds((512,...]
    unnamed x23 -> x0, local copies, waits for them, and re-layouts: 8.88 us -> none
where the time goes in v2:
time: 48.1 us; the launch traced here: 48 us
  Pallas kernels  47.3 us (98%)
  between operations  0.64 us (1%)
    pallas_call x1, Pallas kernels, body(): pl.pallas_call(comm_kernel, out_shape=(sds((512, 512), BF), sds((2, 512),...  46 us
    pallas_call x1, Pallas kernels, body(): pl.pallas_call(finish_kernel, out_shape=(sds((512, 1024), BF), sds((512,...  1.29 us

profile of v2, /device:TPU:1, one launch (start us, length us, event | category | flops | bytes accessed | tf_op | source)
XLA Modules:
  0.0 48.0 jit_solution(13577664611920109312)
XLA Ops:
  0.6 46.0 %adapter_step.1 = (bf16[512,512]{1,0:T(8,128)(2,1)S(1)}, f32[2,512]{1,0:T(2,128)S(1)}, f32[2,64]{1,0:T(2,128)S(1)}, bf16[64,1024]{1,0:T(8,128)(2,1)S(1)}, bf16[6...) custom-call(bf16[512,512]{1,0:T(8,128)(2,1)} %learn_h.1, bf16[512,1024]{1,0:T(8,128)(2,1)} %cot_h.1, ...), custom_call_target="tpu_custom_call" | custom-call | tf_op jit(solution)/shard_map/adapter_step/pallas_call | solution.py:323
  46.7 1.3 %finish.1 = (bf16[512,1024]{1,0:T(8,128)(2,1)}, bf16[512,512]{1,0:T(8,128)(2,1)}, f32[2,512]{1,0:T(2,128)}, f32[2,64]{1,0:T(2,128)}) custom-call(bf16[2,512,512]{2,1,0:T(8,128)(2,1)S(1)} %get-tuple-element.14.m_ref, bf16[64,512]{1,0:T(8,128)(2,1)S(1)} %get-tuple-element.15.ld_ref, bf16[64,1024]{1,0:T(8,128)(2,1)S(1)} %get-tuple-element.16.nut_ref, ...), custom_call_target="tpu_custom_call" | custom-call | tf_op jit(solution)/shard_map/finish/pallas_call | solution.py:357

commit v3 on v2

--- a/solution.py
+++ b/solution.py
@@ -12,6 +12,7 @@
 GZ = 4
 NA = 8
 NB = 4
+NO = 4
 NC = 8
 
 BF = jnp.bfloat16
@@ -35,7 +36,7 @@
     g32, u_send, u_prec, u_sum, u_rs, u_a, u_b, u_fin, upt, nupt16, nup, nu_out,
     m_send, m_keep, m_prec, m_sum, m_rs, m_fin,
     l32, l_send, l_prec, l_all, l_fin,
-    ssem, rsem, lsem,
+    ssem, rsem, rfar, lsem,
 ):
     d = lax.axis_index("dp")
     t = lax.axis_index("tensor")
@@ -61,12 +62,26 @@
     cp_dec = load(dec_h, dec, I_DEC)
     cp_base = load(base_h, base, I_BASE)
 
+    owner = jnp.logical_or(za == 1, za == 2)
+    mine = x * 2 + jnp.where(zb < 2, za - 1, 2 - za)
+
     def near(k):
         other = (a + k) % NA
         return other, {"dp": (other // GZ) * NZ + zb * GZ + other % GZ, "tensor": t}
 
-    def far(k):
-        return {"dp": x * NZ + ((zb + k) % NB) * GZ + za, "tensor": t}
+    def owner_of(o):
+        at = jnp.where(zb < 2, 1 + o % 2, 2 - o % 2)
+        return (o // 2) * GZ + at, {"dp": (o // 2) * NZ + zb * GZ + at, "tensor": t}
+
+    def column(group, at):
+        return {"dp": x * NZ + group * GZ + at, "tensor": t}
+
+    def far_down(k):
+        return column(k, jnp.where((zb < 2) == (k < 2), za, GZ - 1 - za))
+
+    def far_up(k):
+        opposite = jnp.logical_or(zb == k + 2, zb == k - 2)
+        return column(k, jnp.where(opposite, GZ - 1 - za, za))
 
     def chip(k):
         other = (q + k) % NC
@@ -83,18 +98,18 @@
         greet(near(k)[1])
         return 0
 
-    def hello_far(k, _):
-        greet(far(k))
-        return 0
-
     def hello_chip(k, _):
         greet(chip(k)[1])
         return 0
 
-    lax.fori_loop(1, NB, hello_far, 0)
     lax.fori_loop(1, NA, hello_near, 0)
     lax.fori_loop(1, NC, hello_chip, 0)
     greet(pair)
+    for k in range(1, NB):
+        @pl.when(zb < k)
+        def _():
+            greet(column(k, za))
+            greet(column(k, GZ - 1 - za))
 
     def remote(src, dst, i, dev):
         return pltpu.make_async_remote_copy(
@@ -115,11 +130,34 @@
             return 0
         lax.fori_loop(1, NA, step, 0)
 
-    def to_far(i, src, dst):
-        def step(k, _):
-            remote(src, dst, i, far(k)).start()
-            return 0
-        lax.fori_loop(1, NB, step, 0)
+    def send_far(i, dev, buf, k):
+        pltpu.make_async_remote_copy(
+            src_ref=buf.at[zb], dst_ref=buf.at[zb], send_sem=ssem.at[i],
+            recv_sem=rfar.at[i, zb], device_id=dev(k), device_id_type=pl.DeviceIdType.MESH,
+        ).start()
+
+    def far_arrived(i, buf, k):
+        pltpu.make_async_remote_copy(
+            src_ref=buf.at[k], dst_ref=buf.at[k], send_sem=ssem.at[i],
+            recv_sem=rfar.at[i, k], device_id=pair, device_id_type=pl.DeviceIdType.MESH,
+        ).wait_recv()
+
+    def far_down_first(i, dev, buf):
+        for k in range(NB - 1):
+            @pl.when(k < zb)
+            def _():
+                send_far(i, dev, buf, k)
+
+    def far_rest(i, dev, buf):
+        for k in range(1, NB):
+            @pl.when(k > zb)
+            def _():
+                far_arrived(i, buf, k)
+                send_far(i, dev, buf, k)
+        for k in range(NB - 1):
+            @pl.when(k < zb)
+            def _():
+                far_arrived(i, buf, k)
 
     def to_chips(i, src, dst):
         def step(k, _):
@@ -147,13 +185,9 @@
     lowout[...] = dot(cot[...], upt[...].astype(BF), 1, 1).astype(BF)
     cp_learn.wait()
     term = dot(lowout[...], learn[...], 0, 0).astype(BF)
-    for k in range(NA):
-        i, j = k // 4, k % 4
-        td_send[k] = term[32 * i:32 * i + 32, 128 * j:128 * j + 128]
-    d_a[a] = td_send[a]
-
-    pl.semaphore_wait(barrier, (NB - 1) + (NA - 1) + (NC - 1) + 1)
-    to_near(D_A, lambda o: td_send.at[o], d_a.at[a])
+    for k in range(NO):
+        i, j = k // 2, k % 2
+        td_send[k] = term[32 * i:32 * i + 32, 256 * j:256 * j + 256]
 
     cp_down.wait()
     down16 = down[...].astype(BF)
@@ -163,7 +197,23 @@
         for j in range(NC):
             g32[i, j] = term_up[32 * i:32 * i + 32, 128 * j:128 * j + 128]
     u_send[...] = g32[oc].astype(BF)
+
+    pl.semaphore_wait(barrier, (NA - 1) + (NC - 1) + 1 + 2 * zb)
+
+    def to_owner(o, _):
+        place, dev = owner_of(o)
+
+        @pl.when(place != a)
+        def _():
+            remote(td_send.at[o], d_a.at[a], D_A, dev).start()
+        return 0
+
+    lax.fori_loop(0, NO, to_owner, 0)
     remote(u_send, u_prec, U_PAIR, pair).start()
+
+    @pl.when(owner)
+    def _():
+        d_a[a] = td_send[mine]
 
     cp_dec.wait()
     cp_base.wait()
@@ -199,11 +249,13 @@
     lax.fori_loop(0, NC, add_half, 0)
     m_rs[q] = m_sum[q]
 
-    arrived(d_a.at[pl.ds(0, NA - 1)], D_A)
-    d_b[zb] = total_of(d_a).astype(BF)
-    to_far(D_B, d_b.at[zb], d_b.at[zb])
-
     to_chips(M_RS, lambda o: m_sum.at[o], m_rs.at[q])
+
+    @pl.when(owner)
+    def _():
+        arrived(d_a.at[pl.ds(0, NA - 1)], D_A)
+        d_b[zb] = total_of(d_a).astype(BF)
+        far_down_first(D_B, far_down, d_b)
 
     def acts(r, _):
         rows = pl.ds(pl.multiple_of(r * 128, 128), 128)
@@ -221,21 +273,33 @@
 
     arrived(u_a.at[pl.ds(0, NA - 1)], U_A)
     u_b[zb] = total_of(u_a).astype(BF)
-    to_far(U_B, u_b.at[zb], u_b.at[zb])
-
-    arrived(d_b.at[pl.ds(0, NB - 1)], D_B)
-    d_c[a] = total_of(d_b).astype(BF)
-    to_near(D_C, lambda o: d_c.at[a], d_c.at[a])
+    far_down_first(U_B, far_up, u_b)
 
     my_rows = pl.ds(pl.multiple_of(q * 64, 64), 64)
     arrived(m_rs.at[pl.ds(0, NC - 1)], M_RS)
     m_fin[c, my_rows, :] = total_of(m_rs).astype(BF)
     to_chips(M_AG, lambda o: m_fin.at[c, my_rows], m_fin.at[c, my_rows])
 
-    arrived(d_c.at[pl.ds(0, NA - 1)], D_C)
-    for k in range(NA):
-        i, j = k // 4, k % 4
-        rows, cols = pl.ds(32 * i, 32), pl.ds(128 * j, 128)
+    @pl.when(owner)
+    def _():
+        far_rest(D_B, far_down, d_b)
+        d_c[mine] = total_of(d_b).astype(BF)
+        to_near(D_C, lambda o: d_c.at[mine], d_c.at[mine])
+
+    arrived(m_fin.at[c, pl.ds(0, 448)], M_AG)
+    remote(m_fin.at[c], m_fin.at[c], M_PAIR2, pair).start()
+
+    @pl.when(owner)
+    def _():
+        arrived(d_c.at[pl.ds(0, NO - 1)], D_C)
+
+    @pl.when(jnp.logical_not(owner))
+    def _():
+        arrived(d_c, D_C)
+
+    for k in range(NO):
+        i, j = k // 2, k % 2
+        rows, cols = pl.ds(32 * i, 32), pl.ds(256 * j, 256)
         grad = d_c[k].astype(F32) / total
         ndown[rows, cols] = down[rows, cols] - rate_down * grad
     l32[...] = dot(ndown[...].astype(BF), dec[...], 1, 1)
@@ -247,12 +311,9 @@
     l_all[q] = (l32[pl.ds(pl.multiple_of(c * 32, 32), 32), :] + l_prec[...].astype(F32)).astype(BF)
     to_chips(L_ALL, lambda o: l_all.at[q], l_all.at[q])
 
-    arrived(u_b.at[pl.ds(0, NB - 1)], U_B)
+    far_rest(U_B, far_up, u_b)
     u_fin[c, q] = total_of(u_b).astype(BF)
     to_chips(U_AG, lambda o: u_fin.at[c, q], u_fin.at[c, q])
-
-    arrived(m_fin.at[c, pl.ds(0, 448)], M_AG)
-    remote(m_fin.at[c], m_fin.at[c], M_PAIR2, pair).start()
 
     arrived(u_fin.at[c, pl.ds(0, NC - 1)], U_AG)
     remote(u_fin.at[c], u_fin.at[c], U_PAIR2, pair).start()
@@ -268,8 +329,9 @@
             upt[rows, cols] = upt[rows, cols] - rate_up * grad
     nupt16[...] = upt[...].astype(BF)
     cp_nut = load(nupt16, nut_h, O_NUT)
-    nup[...] = upt[...].T
-    nu_out[...] = two_rows(nup, d * 4 + t // 4, 2 * (t % 4))
+    first = d * 32 + t * 2
+    nup[...] = upt[:, pl.ds(pl.multiple_of(first // 128 * 128, 128), 128)].T
+    nu_out[...] = two_rows(nup, first % 128 // 8, first % 8)
     cp_nu = load(nu_out, nu_h, O_NU)
 
     half = pl.ds(pl.multiple_of(c * 32, 32), 32)
@@ -281,14 +343,24 @@
 
     m_part = m_fin.at[c, pl.ds(0, 448)]
     for ref, i in (
-        (td_send.at[pl.ds(0, NA - 1)], D_A), (d_b.at[pl.ds(0, NB - 1)], D_B),
-        (d_c.at[pl.ds(0, NA - 1)], D_C), (u_send, U_PAIR), (u_rs.at[pl.ds(0, NC - 1)], U_RS),
+        (u_send, U_PAIR), (u_rs.at[pl.ds(0, NC - 1)], U_RS),
         (u_a.at[pl.ds(0, NA - 1)], U_A), (u_b.at[pl.ds(0, NB - 1)], U_B),
         (u_fin.at[c, pl.ds(0, NC - 1)], U_AG), (u_fin.at[c], U_PAIR2), (m_send, M_PAIR),
         (m_rs.at[pl.ds(0, NC - 1)], M_RS), (m_part, M_AG), (m_fin.at[c], M_PAIR2),
         (l_send, L_PAIR), (l_all.at[pl.ds(0, NC - 1)], L_ALL), (l_fin.at[half], L_PAIR2),
     ):
         sent(ref, i)
+
+    @pl.when(owner)
+    def _():
+        sent(td_send.at[pl.ds(0, NO - 1)], D_A)
+        sent(d_b.at[pl.ds(0, NB - 1)], D_B)
+        sent(d_a.at[pl.ds(0, NA - 1)], D_C)
+
+    @pl.when(jnp.logical_not(owner))
+    def _():
+        sent(td_send, D_A)
+
     for cp in (cp_ga, cp_nd, cp_m, cp_nut, cp_nu, cp_ld):
         cp.wait()
 
@@ -331,17 +403,18 @@
         scratch_shapes=[
             V((512, 512), BF), V((512, 1024), BF), V((512, 1024), BF), V((64, 512), F32),
             V((512, 512), BF), V((512, 512), BF),
-            V((512, 64), BF), V((NA, 32, 128), BF), V((NA, 32, 128), BF), V((NB, 32, 128), BF),
-            V((NA, 32, 128), BF), V((64, 512), F32), V((2, 512), F32),
+            V((512, 64), BF), V((NO, 32, 256), BF), V((NA, 32, 256), BF), V((NB, 32, 256), BF),
+            V((NO, 32, 256), BF), V((64, 512), F32), V((2, 512), F32),
             V((2, NC, 32, 128), F32), V((NC, 32, 128), BF), V((NC, 32, 128), BF),
             V((NC, 32, 128), BF), V((NC, 32, 128), BF), V((NA, 32, 128), BF), V((NB, 32, 128), BF),
-            V((2, NC, 32, 128), BF), V((64, 1024), F32), V((64, 1024), BF), V((1024, 64), F32),
+            V((2, NC, 32, 128), BF), V((64, 1024), F32), V((64, 1024), BF), V((128, 64), F32),
             V((2, 64), F32),
             V((512, 512), BF), V((512, 512), F32), V((512, 512), BF), V((NC, 64, 512), BF),
             V((NC, 64, 512), BF), V((2, 512, 512), BF),
             V((64, 512), F32), V((32, 512), BF), V((32, 512), BF), V((NC, 32, 512), BF),
             V((64, 512), BF),
             pltpu.SemaphoreType.DMA((16,)), pltpu.SemaphoreType.DMA((16,)),
+            pltpu.SemaphoreType.DMA((16, NB)),
             pltpu.SemaphoreType.DMA((12,)),
         ],
         compiler_params=pltpu.CompilerParams(

time: 48.1 us -> 45.5 us (0.946)
  Pallas kernels: 47.3 us -> 44.8 us
    pallas_call x1, Pallas kernels: 46 us -> 43.5 us  [body(): pl.pallas_call(comm_kernel, out_shape=(sds((512, 512), BF), sds((2, 512),...]
where the time goes in v3:
time: 45.5 us; the launch traced here: 45.4 us
  Pallas kernels  44.8 us (98%)
  between operations  0.64 us (1%)
    pallas_call x1, Pallas kernels, body(): pl.pallas_call(comm_kernel, out_shape=(sds((512, 512), BF), sds((2, 512),...  43.5 us
    pallas_call x1, Pallas kernels, body(): pl.pallas_call(finish_kernel, out_shape=(sds((512, 1024), BF), sds((512,...  1.28 us

profile of v3, /device:TPU:1, one launch (start us, length us, event | category | flops | bytes accessed | tf_op | source)
XLA Modules:
  0.0 45.4 jit_solution(14893109482019130091)
XLA Ops:
  0.6 43.5 %adapter_step.1 = (bf16[512,512]{1,0:T(8,128)(2,1)S(1)}, f32[2,512]{1,0:T(2,128)S(1)}, f32[2,64]{1,0:T(2,128)S(1)}, bf16[64,1024]{1,0:T(8,128)(2,1)S(1)}, bf16[6...) custom-call(bf16[512,512]{1,0:T(8,128)(2,1)} %learn_h.1, bf16[512,1024]{1,0:T(8,128)(2,1)} %cot_h.1, ...), custom_call_target="tpu_custom_call" | custom-call | tf_op jit(solution)/shard_map/adapter_step/pallas_call | solution.py:395
  44.1 1.3 %finish.1 = (bf16[512,1024]{1,0:T(8,128)(2,1)}, bf16[512,512]{1,0:T(8,128)(2,1)}, f32[2,512]{1,0:T(2,128)}, f32[2,64]{1,0:T(2,128)}) custom-call(bf16[2,512,512]{2,1,0:T(8,128)(2,1)S(1)} %get-tuple-element.14.m_ref, bf16[64,512]{1,0:T(8,128)(2,1)S(1)} %get-tuple-element.15.ld_ref, bf16[64,1024]{1,0:T(8,128)(2,1)S(1)} %get-tuple-element.16.nut_ref, ...), custom_call_target="tpu_custom_call" | custom-call | tf_op jit(solution)/shard_map/finish/pallas_call | solution.py:430

commit v4 on v3

--- a/solution.py
+++ b/solution.py
@@ -20,8 +20,7 @@
 
 (D_A, D_B, D_C, U_PAIR, U_RS, U_A, U_B, U_AG, U_PAIR2,
  M_PAIR, M_RS, M_AG, M_PAIR2, L_PAIR, L_ALL, L_PAIR2) = range(16)
-(I_COT, I_UP, I_LEARN, I_DOWN, I_DEC, I_BASE,
- O_GA, O_ND, O_NU, O_NUT, O_LD, O_M) = range(12)
+(I_COT, I_UP, I_LEARN, I_DOWN, I_DEC, I_BASE, O_M) = range(7)
 
 
 def dot(a, b, ca, cb):
@@ -30,13 +29,13 @@
 
 def comm_kernel(
     learn_h, cot_h, base_h, down_h, up_h, dec_h,
-    ga_h, nd_h, nu_h, nut_h, ld_h, m_h,
-    learn, cot, base, down, dec, ga,
-    lowout, td_send, d_a, d_b, d_c, ndown, nd_out,
-    g32, u_send, u_prec, u_sum, u_rs, u_a, u_b, u_fin, upt, nupt16, nup, nu_out,
+    ga, nd_out, nu_out, nupt16, l_fin, m_h,
+    learn, cot, base, down, dec,
+    lowout, td_send, d_a, d_b, d_c, ndown,
+    g32, u_send, u_prec, u_sum, u_rs, u_a, u_b, u_fin, upt, nup,
     m_send, m_keep, m_prec, m_sum, m_rs, m_fin,
-    l32, l_send, l_prec, l_all, l_fin,
-    ssem, rsem, rfar, lsem,
+    l32, l_send, l_prec, l_all,
+    ssem, rsem, rfar, lsem, entered,
 ):
     d = lax.axis_index("dp")
     t = lax.axis_index("tensor")
@@ -55,10 +54,10 @@
         cp.start()
         return cp
 
+    cp_down = load(down_h, down, I_DOWN)
+    cp_learn = load(learn_h, learn, I_LEARN)
+    cp_up = load(up_h, upt, I_UP)
     cp_cot = load(cot_h, cot, I_COT)
-    cp_up = load(up_h, upt, I_UP)
-    cp_learn = load(learn_h, learn, I_LEARN)
-    cp_down = load(down_h, down, I_DOWN)
     cp_dec = load(dec_h, dec, I_DEC)
     cp_base = load(base_h, base, I_BASE)
 
@@ -142,22 +141,17 @@
             recv_sem=rfar.at[i, k], device_id=pair, device_id_type=pl.DeviceIdType.MESH,
         ).wait_recv()
 
-    def far_down_first(i, dev, buf):
-        for k in range(NB - 1):
-            @pl.when(k < zb)
+    def far_send(i, dev, buf, wanted):
+        for step in (1, 3, 2):
+            k = (zb + step) % NB
+
+            @pl.when(k > zb if wanted == "higher" else k < zb)
             def _():
                 send_far(i, dev, buf, k)
 
-    def far_rest(i, dev, buf):
-        for k in range(1, NB):
-            @pl.when(k > zb)
-            def _():
-                far_arrived(i, buf, k)
-                send_far(i, dev, buf, k)
-        for k in range(NB - 1):
-            @pl.when(k < zb)
-            def _():
-                far_arrived(i, buf, k)
+    def far_wait(i, buf):
+        for step in range(1, NB):
+            far_arrived(i, buf, (zb + step) % NB)
 
     def to_chips(i, src, dst):
         def step(k, _):
@@ -180,35 +174,42 @@
         ]
         return jnp.concatenate(picked, axis=0)
 
+    cp_down.wait()
+    cp_learn.wait()
+    low_in = dot(down[...].astype(BF), learn[...], 1, 1).astype(BF)
+    cp_up.wait()
     cp_cot.wait()
-    cp_up.wait()
     lowout[...] = dot(cot[...], upt[...].astype(BF), 1, 1).astype(BF)
-    cp_learn.wait()
     term = dot(lowout[...], learn[...], 0, 0).astype(BF)
     for k in range(NO):
         i, j = k // 2, k % 2
         td_send[k] = term[32 * i:32 * i + 32, 256 * j:256 * j + 256]
 
-    cp_down.wait()
-    down16 = down[...].astype(BF)
-    low_in = dot(down16, learn[...], 1, 1).astype(BF)
+    pl.semaphore_wait(barrier, (NA - 1) + (NC - 1) + 1 + 2 * zb)
+
+    def to_owner(o, _):
+        place, dev = owner_of(o)
+
+        @pl.when(place != a)
+        def _():
+            remote(td_send.at[o], d_a.at[a], D_A, dev).start()
+        return 0
+
+    lax.fori_loop(0, NO, to_owner, 0)
+
+    for k in range(NB - 1):
+        @pl.when(k < zb)
+        def _():
+            for at in (za, GZ - 1 - za):
+                pl.semaphore_signal(
+                    entered, inc=1, device_id=column(k, at), device_id_type=pl.DeviceIdType.MESH
+                )
+
     term_up = dot(low_in, cot[...], 1, 0)
     for i in range(2):
         for j in range(NC):
             g32[i, j] = term_up[32 * i:32 * i + 32, 128 * j:128 * j + 128]
     u_send[...] = g32[oc].astype(BF)
-
-    pl.semaphore_wait(barrier, (NA - 1) + (NC - 1) + 1 + 2 * zb)
-
-    def to_owner(o, _):
-        place, dev = owner_of(o)
-
-        @pl.when(place != a)
-        def _():
-            remote(td_send.at[o], d_a.at[a], D_A, dev).start()
-        return 0
-
-    lax.fori_loop(0, NO, to_owner, 0)
     remote(u_send, u_prec, U_PAIR, pair).start()
 
     @pl.when(owner)
@@ -219,18 +220,18 @@
     cp_base.wait()
 
     def other_half(r, _):
-        rows = pl.ds(pl.multiple_of(r * 128, 128), 128)
-        cols = pl.ds(pl.multiple_of(oc * 512, 512), 512)
-        m_send[rows, :] = dot(dec[rows, :], base[:, cols], 1, 0).astype(BF)
+        to = pl.ds(pl.multiple_of(r * 256, 256), 256)
+        cols = pl.ds(pl.multiple_of(oc * 512 + r * 256, 256), 256)
+        m_send[:, to] = dot(dec[...], base[:, cols], 1, 0).astype(BF)
         return 0
 
     def own_half(r, _):
-        rows = pl.ds(pl.multiple_of(r * 128, 128), 128)
-        cols = pl.ds(pl.multiple_of(c * 512, 512), 512)
-        m_keep[rows, :] = dot(dec[rows, :], base[:, cols], 1, 0)
-        return 0
-
-    lax.fori_loop(0, 4, other_half, 0)
+        to = pl.ds(pl.multiple_of(r * 256, 256), 256)
+        cols = pl.ds(pl.multiple_of(c * 512 + r * 256, 256), 256)
+        m_keep[:, to] = dot(dec[...], base[:, cols], 1, 0)
+        return 0
+
+    lax.fori_loop(0, 2, other_half, 0)
     remote(m_send, m_prec, M_PAIR, pair).start()
 
     arrived(u_prec, U_PAIR)
@@ -238,7 +239,7 @@
     u_rs[q] = u_sum[q]
     to_chips(U_RS, lambda o: u_sum.at[o], u_rs.at[q])
 
-    lax.fori_loop(0, 4, own_half, 0)
+    lax.fori_loop(0, 2, own_half, 0)
     arrived(m_prec, M_PAIR)
 
     def add_half(r, _):
@@ -255,17 +256,7 @@
     def _():
         arrived(d_a.at[pl.ds(0, NA - 1)], D_A)
         d_b[zb] = total_of(d_a).astype(BF)
-        far_down_first(D_B, far_down, d_b)
-
-    def acts(r, _):
-        rows = pl.ds(pl.multiple_of(r * 128, 128), 128)
-        ga[rows, :] = (
-            dot(cot[rows, :], base[...], 1, 1) + dot(lowout[rows, :], down[...].astype(BF), 1, 0)
-        ).astype(BF)
-        return 0
-
-    lax.fori_loop(0, 4, acts, 0)
-    cp_ga = load(ga, ga_h, O_GA)
+        far_send(D_B, far_down, d_b, "lower")
 
     arrived(u_rs.at[pl.ds(0, NC - 1)], U_RS)
     u_a[a] = total_of(u_rs).astype(BF)
@@ -273,21 +264,37 @@
 
     arrived(u_a.at[pl.ds(0, NA - 1)], U_A)
     u_b[zb] = total_of(u_a).astype(BF)
-    far_down_first(U_B, far_up, u_b)
+    far_send(U_B, far_up, u_b, "lower")
 
     my_rows = pl.ds(pl.multiple_of(q * 64, 64), 64)
     arrived(m_rs.at[pl.ds(0, NC - 1)], M_RS)
     m_fin[c, my_rows, :] = total_of(m_rs).astype(BF)
     to_chips(M_AG, lambda o: m_fin.at[c, my_rows], m_fin.at[c, my_rows])
 
-    @pl.when(owner)
-    def _():
-        far_rest(D_B, far_down, d_b)
+    @pl.when(zb < NB - 1)
+    def _():
+        pl.semaphore_wait(entered, 2 * (NB - 1 - zb))
+
+    @pl.when(owner)
+    def _():
+        far_send(D_B, far_down, d_b, "higher")
+
+    far_send(U_B, far_up, u_b, "higher")
+
+    def acts(r, _):
+        cols = pl.ds(pl.multiple_of(r * 256, 256), 256)
+        ga[:, cols] = (
+            dot(cot[...], base[cols, :], 1, 1) + dot(lowout[...], down[:, cols].astype(BF), 1, 0)
+        ).astype(BF)
+        return 0
+
+    lax.fori_loop(0, 2, acts, 0)
+
+    @pl.when(owner)
+    def _():
+        far_wait(D_B, d_b)
         d_c[mine] = total_of(d_b).astype(BF)
         to_near(D_C, lambda o: d_c.at[mine], d_c.at[mine])
-
-    arrived(m_fin.at[c, pl.ds(0, 448)], M_AG)
-    remote(m_fin.at[c], m_fin.at[c], M_PAIR2, pair).start()
 
     @pl.when(owner)
     def _():
@@ -306,40 +313,40 @@
     l_send[...] = l32[pl.ds(pl.multiple_of(oc * 32, 32), 32), :].astype(BF)
     remote(l_send, l_prec, L_PAIR, pair).start()
     nd_out[...] = two_rows(ndown, d // 4, 2 * (d % 4))
-    cp_nd = load(nd_out, nd_h, O_ND)
     arrived(l_prec, L_PAIR)
     l_all[q] = (l32[pl.ds(pl.multiple_of(c * 32, 32), 32), :] + l_prec[...].astype(F32)).astype(BF)
     to_chips(L_ALL, lambda o: l_all.at[q], l_all.at[q])
 
-    far_rest(U_B, far_up, u_b)
+    far_wait(U_B, u_b)
     u_fin[c, q] = total_of(u_b).astype(BF)
     to_chips(U_AG, lambda o: u_fin.at[c, q], u_fin.at[c, q])
 
+    arrived(m_fin.at[c, pl.ds(0, 448)], M_AG)
+    remote(m_fin.at[c], m_fin.at[c], M_PAIR2, pair).start()
+    arrived(m_fin.at[oc], M_PAIR2)
+    cp_m = load(m_fin, m_h, O_M)
+
     arrived(u_fin.at[c, pl.ds(0, NC - 1)], U_AG)
     remote(u_fin.at[c], u_fin.at[c], U_PAIR2, pair).start()
 
-    arrived(m_fin.at[oc], M_PAIR2)
-    cp_m = load(m_fin, m_h, O_M)
+    half = pl.ds(pl.multiple_of(c * 32, 32), 32)
+    arrived(l_all.at[pl.ds(0, NC - 1)], L_ALL)
+    l_fin[half, :] = total_of(l_all).astype(BF)
+    remote(l_fin.at[half], l_fin.at[half], L_PAIR2, pair).start()
 
     arrived(u_fin.at[oc], U_PAIR2)
     for i in range(2):
         for j in range(NC):
             rows, cols = pl.ds(32 * i, 32), pl.ds(128 * j, 128)
             grad = u_fin[i, j].astype(F32) / total
-            upt[rows, cols] = upt[rows, cols] - rate_up * grad
-    nupt16[...] = upt[...].astype(BF)
-    cp_nut = load(nupt16, nut_h, O_NUT)
+            new = upt[rows, cols] - rate_up * grad
+            upt[rows, cols] = new
+            nupt16[rows, cols] = new.astype(BF)
     first = d * 32 + t * 2
     nup[...] = upt[:, pl.ds(pl.multiple_of(first // 128 * 128, 128), 128)].T
     nu_out[...] = two_rows(nup, first % 128 // 8, first % 8)
-    cp_nu = load(nu_out, nu_h, O_NU)
-
-    half = pl.ds(pl.multiple_of(c * 32, 32), 32)
-    arrived(l_all.at[pl.ds(0, NC - 1)], L_ALL)
-    l_fin[half, :] = total_of(l_all).astype(BF)
-    remote(l_fin.at[half], l_fin.at[half], L_PAIR2, pair).start()
+
     arrived(l_fin.at[half], L_PAIR2)
-    cp_ld = load(l_fin, ld_h, O_LD)
 
     m_part = m_fin.at[c, pl.ds(0, 448)]
     for ref, i in (
@@ -361,8 +368,7 @@
     def _():
         sent(td_send, D_A)
 
-    for cp in (cp_ga, cp_nd, cp_m, cp_nut, cp_nu, cp_ld):
-        cp.wait()
+    cp_m.wait()
 
 
 def finish_kernel(m_ref, ld_ref, nut_ref, ga_ref, nd_ref, nu_ref, dec_h, ga_h, nd_h, nu_h, dec_v, sem):
@@ -399,23 +405,21 @@
             sds((64, 1024), BF), sds((64, 512), BF), sds((2, 512, 512), BF),
         ),
         in_specs=[hbm] * 6,
-        out_specs=(any_,) * 6,
+        out_specs=(vmem,) * 5 + (any_,),
         scratch_shapes=[
             V((512, 512), BF), V((512, 1024), BF), V((512, 1024), BF), V((64, 512), F32),
-            V((512, 512), BF), V((512, 512), BF),
+            V((512, 512), BF),
             V((512, 64), BF), V((NO, 32, 256), BF), V((NA, 32, 256), BF), V((NB, 32, 256), BF),
-            V((NO, 32, 256), BF), V((64, 512), F32), V((2, 512), F32),
+            V((NO, 32, 256), BF), V((64, 512), F32),
             V((2, NC, 32, 128), F32), V((NC, 32, 128), BF), V((NC, 32, 128), BF),
             V((NC, 32, 128), BF), V((NC, 32, 128), BF), V((NA, 32, 128), BF), V((NB, 32, 128), BF),
-            V((2, NC, 32, 128), BF), V((64, 1024), F32), V((64, 1024), BF), V((128, 64), F32),
-            V((2, 64), F32),
+            V((2, NC, 32, 128), BF), V((64, 1024), F32), V((128, 64), F32),
             V((512, 512), BF), V((512, 512), F32), V((512, 512), BF), V((NC, 64, 512), BF),
             V((NC, 64, 512), BF), V((2, 512, 512), BF),
             V((64, 512), F32), V((32, 512), BF), V((32, 512), BF), V((NC, 32, 512), BF),
-            V((64, 512), BF),
             pltpu.SemaphoreType.DMA((16,)), pltpu.SemaphoreType.DMA((16,)),
             pltpu.SemaphoreType.DMA((16, NB)),
-            pltpu.SemaphoreType.DMA((12,)),
+            pltpu.SemaphoreType.DMA((7,)), pltpu.SemaphoreType.REGULAR,
         ],
         compiler_params=pltpu.CompilerParams(
             collective_id=0, has_side_effects=True, vmem_limit_bytes=48 * 1024 * 1024

time: 45.5 us -> 43.1 us (0.947)
  Pallas kernels: 44.8 us -> 42.4 us
    pallas_call x1, Pallas kernels: 43.5 us -> 41.1 us  [body(): pl.pallas_call(comm_kernel, out_shape=(sds((512, 512), BF), sds((2, 512),...]
where the time goes in v4:
time: 43.1 us; the launch traced here: 43 us
  Pallas kernels  42.4 us (98%)
  between operations  0.64 us (1%)
    pallas_call x1, Pallas kernels, body(): pl.pallas_call(comm_kernel, out_shape=(sds((512, 512), BF), sds((2, 512),...  41.1 us
    pallas_call x1, Pallas kernels, body(): pl.pallas_call(finish_kernel, out_shape=(sds((512, 1024), BF), sds((512,...  1.29 us

profile of v4, /device:TPU:1, one launch (start us, length us, event | category | flops | bytes accessed | tf_op | source)
XLA Modules:
  0.0 43.0 jit_solution(11636843610326133444)
XLA Ops:
  0.6 41.1 %adapter_step.1 = (bf16[512,512]{1,0:T(8,128)(2,1)S(1)}, f32[2,512]{1,0:T(2,128)S(1)}, f32[2,64]{1,0:T(2,128)S(1)}, bf16[64,1024]{1,0:T(8,128)(2,1)S(1)}, bf16[6...) custom-call(bf16[512,512]{1,0:T(8,128)(2,1)} %learn_h.1, bf16[512,1024]{1,0:T(8,128)(2,1)} %cot_h.1, ...), custom_call_target="tpu_custom_call" | custom-call | tf_op jit(solution)/shard_map/adapter_step/pallas_call | solution.py:401
  41.7 1.3 %finish.1 = (bf16[512,1024]{1,0:T(8,128)(2,1)}, bf16[512,512]{1,0:T(8,128)(2,1)}, f32[2,512]{1,0:T(2,128)}, f32[2,64]{1,0:T(2,128)}) custom-call(bf16[2,512,512]{2,1,0:T(8,128)(2,1)S(1)} %get-tuple-element.14.m_ref, bf16[64,512]{1,0:T(8,128)(2,1)S(1)} %get-tuple-element.15.ld_ref, bf16[64,1024]{1,0:T(8,128)(2,1)S(1)} %get-tuple-element.16.nut_ref, ...), custom_call_target="tpu_custom_call" | custom-call | tf_op jit(solution)/shard_map/finish/pallas_call | solution.py:434

commit v5 on v4

--- a/solution.py
+++ b/solution.py
@@ -14,12 +14,13 @@
 NB = 4
 NO = 4
 NC = 8
+NW = 16
 
 BF = jnp.bfloat16
 F32 = jnp.float32
 
 (D_A, D_B, D_C, U_PAIR, U_RS, U_A, U_B, U_AG, U_PAIR2,
- M_PAIR, M_RS, M_AG, M_PAIR2, L_PAIR, L_ALL, L_PAIR2) = range(16)
+ M_PAIR, M_RS, M_AG, M_PAIR2, DEC_PAIR, L_ALL, L_PAIR2, DOWN_PAIR, ND_PAIR) = range(18)
 (I_COT, I_UP, I_LEARN, I_DOWN, I_DEC, I_BASE, O_M) = range(7)
 
 
@@ -30,11 +31,10 @@
 def comm_kernel(
     learn_h, cot_h, base_h, down_h, up_h, dec_h,
     ga, nd_out, nu_out, nupt16, l_fin, m_h,
-    learn, cot, base, down, dec,
-    lowout, td_send, d_a, d_b, d_c, ndown,
-    g32, u_send, u_prec, u_sum, u_rs, u_a, u_b, u_fin, upt, nup,
-    m_send, m_keep, m_prec, m_sum, m_rs, m_fin,
-    l32, l_send, l_prec, l_all,
+    learn, cot, base, down, dec, dec_p, down_p,
+    lowout, low_in, td_send, d_a, d_b, d_o, d_c, ndown, ndown_p, nd_send, nd_prec,
+    u_send, u_prec, u_sum, u_rs, u_a, u_b, u_fin, upt, nup,
+    m_send, m_keep, m_prec, m_sum, m_rs, m_fin, l_all,
     ssem, rsem, rfar, lsem, entered,
 ):
     d = lax.axis_index("dp")
@@ -47,6 +47,7 @@
     q = t // 2
     c = t % 2
     oc = 1 - c
+    w = x * NC + q
     total = 16384.0
 
     def load(src, dst, i):
@@ -68,6 +69,9 @@
         other = (a + k) % NA
         return other, {"dp": (other // GZ) * NZ + zb * GZ + other % GZ, "tensor": t}
 
+    def near_core(k, core):
+        return {"dp": near(k)[1]["dp"], "tensor": q * 2 + core}
+
     def owner_of(o):
         at = jnp.where(zb < 2, 1 + o % 2, 2 - o % 2)
         return (o // 2) * GZ + at, {"dp": (o // 2) * NZ + zb * GZ + at, "tensor": t}
@@ -82,6 +86,13 @@
         opposite = jnp.logical_or(zb == k + 2, zb == k - 2)
         return column(k, jnp.where(opposite, GZ - 1 - za, za))
 
+    def wide(k):
+        other = (w + k) % NW
+        return other, {"dp": (other // NC) * NZ + z, "tensor": (other % NC) * 2 + c}
+
+    def above(k):
+        return {"dp": x * NZ + zb * GZ + (za + k) % GZ, "tensor": t}
+
     def chip(k):
         other = (q + k) % NC
         return other, {"dp": d, "tensor": other * 2 + c}
@@ -94,15 +105,16 @@
         pl.semaphore_signal(barrier, inc=1, device_id=dev, device_id_type=pl.DeviceIdType.MESH)
 
     def hello_near(k, _):
-        greet(near(k)[1])
-        return 0
-
-    def hello_chip(k, _):
-        greet(chip(k)[1])
+        for core in range(2):
+            greet(near_core(k, core))
+        return 0
+
+    def hello_wide(k, _):
+        greet(wide(k)[1])
         return 0
 
     lax.fori_loop(1, NA, hello_near, 0)
-    lax.fori_loop(1, NC, hello_chip, 0)
+    lax.fori_loop(1, NW, hello_wide, 0)
     greet(pair)
     for k in range(1, NB):
         @pl.when(zb < k)
@@ -122,12 +134,12 @@
     def sent(ref, i):
         remote(ref, ref, i, pair).wait_send()
 
-    def to_near(i, src, dst):
+    def each(n, place, i, src, dst):
         def step(k, _):
-            other, dev = near(k)
+            other, dev = place(k)
             remote(src(other), dst, i, dev).start()
             return 0
-        lax.fori_loop(1, NA, step, 0)
+        lax.fori_loop(1, n, step, 0)
 
     def send_far(i, dev, buf, k):
         pltpu.make_async_remote_copy(
@@ -152,13 +164,6 @@
     def far_wait(i, buf):
         for step in range(1, NB):
             far_arrived(i, buf, (zb + step) % NB)
-
-    def to_chips(i, src, dst):
-        def step(k, _):
-            other, dev = chip(k)
-            remote(src(other), dst, i, dev).start()
-            return 0
-        lax.fori_loop(1, NC, step, 0)
 
     def total_of(ref):
         acc = ref[0].astype(F32)
@@ -176,7 +181,10 @@
 
     cp_down.wait()
     cp_learn.wait()
-    low_in = dot(down[...].astype(BF), learn[...], 1, 1).astype(BF)
+    low_in[...] = dot(down[...].astype(BF), learn[...], 1, 1)
+    own = pl.ds(pl.multiple_of(c * 32, 32), 32)
+    theirs = pl.ds(pl.multiple_of(oc * 32, 32), 32)
+    u_send[...] = low_in[theirs, :].astype(BF)
     cp_up.wait()
     cp_cot.wait()
     lowout[...] = dot(cot[...], upt[...].astype(BF), 1, 1).astype(BF)
@@ -185,7 +193,9 @@
         i, j = k // 2, k % 2
         td_send[k] = term[32 * i:32 * i + 32, 256 * j:256 * j + 256]
 
-    pl.semaphore_wait(barrier, (NA - 1) + (NC - 1) + 1 + 2 * zb)
+    pl.semaphore_wait(barrier, 2 * (NA - 1) + (NW - 1) + 1 + 2 * zb)
+
+    remote(u_send, u_prec, U_PAIR, pair).start()
 
     def to_owner(o, _):
         place, dev = owner_of(o)
@@ -205,13 +215,6 @@
                     entered, inc=1, device_id=column(k, at), device_id_type=pl.DeviceIdType.MESH
                 )
 
-    term_up = dot(low_in, cot[...], 1, 0)
-    for i in range(2):
-        for j in range(NC):
-            g32[i, j] = term_up[32 * i:32 * i + 32, 128 * j:128 * j + 128]
-    u_send[...] = g32[oc].astype(BF)
-    remote(u_send, u_prec, U_PAIR, pair).start()
-
     @pl.when(owner)
     def _():
         d_a[a] = td_send[mine]
@@ -235,9 +238,16 @@
     remote(m_send, m_prec, M_PAIR, pair).start()
 
     arrived(u_prec, U_PAIR)
-    u_sum[...] = (g32[c] + u_prec[...].astype(F32)).astype(BF)
-    u_rs[q] = u_sum[q]
-    to_chips(U_RS, lambda o: u_sum.at[o], u_rs.at[q])
+    pair_in = (low_in[own, :] + u_prec[...].astype(F32)).astype(BF)
+    term_up = dot(pair_in, cot[...], 1, 0).astype(BF)
+    for i in range(2):
+        for j in range(NC):
+            u_sum[i * NC + j] = term_up[16 * i:16 * i + 16, 128 * j:128 * j + 128]
+    u_rs[w] = u_sum[w]
+    each(NW, wide, U_RS, lambda o: u_sum.at[o], u_rs.at[w])
+
+    remote(dec, dec_p, DEC_PAIR, pair).start()
+    remote(down.at[theirs], down_p, DOWN_PAIR, pair).start()
 
     lax.fori_loop(0, 2, own_half, 0)
     arrived(m_prec, M_PAIR)
@@ -250,7 +260,7 @@
     lax.fori_loop(0, NC, add_half, 0)
     m_rs[q] = m_sum[q]
 
-    to_chips(M_RS, lambda o: m_sum.at[o], m_rs.at[q])
+    each(NC, chip, M_RS, lambda o: m_sum.at[o], m_rs.at[q])
 
     @pl.when(owner)
     def _():
@@ -258,18 +268,19 @@
         d_b[zb] = total_of(d_a).astype(BF)
         far_send(D_B, far_down, d_b, "lower")
 
-    arrived(u_rs.at[pl.ds(0, NC - 1)], U_RS)
-    u_a[a] = total_of(u_rs).astype(BF)
-    to_near(U_A, lambda o: u_a.at[a], u_a.at[a])
-
-    arrived(u_a.at[pl.ds(0, NA - 1)], U_A)
+    arrived(u_rs.at[pl.ds(0, NW - 1)], U_RS)
+    u_a[za] = total_of(u_rs).astype(BF)
+    for k in range(1, GZ):
+        remote(u_a.at[za], u_a.at[za], U_A, above(k)).start()
+
+    arrived(u_a.at[pl.ds(0, GZ - 1)], U_A)
     u_b[zb] = total_of(u_a).astype(BF)
     far_send(U_B, far_up, u_b, "lower")
 
     my_rows = pl.ds(pl.multiple_of(q * 64, 64), 64)
     arrived(m_rs.at[pl.ds(0, NC - 1)], M_RS)
     m_fin[c, my_rows, :] = total_of(m_rs).astype(BF)
-    to_chips(M_AG, lambda o: m_fin.at[c, my_rows], m_fin.at[c, my_rows])
+    each(NC, chip, M_AG, lambda o: m_fin.at[c, my_rows], m_fin.at[c, my_rows])
 
     @pl.when(zb < NB - 1)
     def _():
@@ -293,52 +304,76 @@
     @pl.when(owner)
     def _():
         far_wait(D_B, d_b)
-        d_c[mine] = total_of(d_b).astype(BF)
-        to_near(D_C, lambda o: d_c.at[mine], d_c.at[mine])
-
-    @pl.when(owner)
+        d_o[...] = total_of(d_b).astype(BF)
+        slot = c * 2 + mine % 2
+
+        def to_core(k, _):
+            remote(d_o, d_c.at[slot], D_C, near_core(k, x)).start()
+            return 0
+
+        lax.fori_loop(1, NA, to_core, 0)
+
+        @pl.when(x == c)
+        def _():
+            d_c[slot] = d_o[...]
+
+        @pl.when(x != c)
+        def _():
+            remote(d_o, d_c.at[slot], D_C, pair).start()
+
+    arrived(dec_p, DEC_PAIR)
+    arrived(down_p, DOWN_PAIR)
+    holds = jnp.logical_and(owner, x == c)
+
+    @pl.when(holds)
     def _():
         arrived(d_c.at[pl.ds(0, NO - 1)], D_C)
 
-    @pl.when(jnp.logical_not(owner))
+    @pl.when(jnp.logical_not(holds))
     def _():
         arrived(d_c, D_C)
 
-    for k in range(NO):
-        i, j = k // 2, k % 2
-        rows, cols = pl.ds(32 * i, 32), pl.ds(256 * j, 256)
-        grad = d_c[k].astype(F32) / total
-        ndown[rows, cols] = down[rows, cols] - rate_down * grad
-    l32[...] = dot(ndown[...].astype(BF), dec[...], 1, 1)
-    l_send[...] = l32[pl.ds(pl.multiple_of(oc * 32, 32), 32), :].astype(BF)
-    remote(l_send, l_prec, L_PAIR, pair).start()
-    nd_out[...] = two_rows(ndown, d // 4, 2 * (d % 4))
-    arrived(l_prec, L_PAIR)
-    l_all[q] = (l32[pl.ds(pl.multiple_of(c * 32, 32), 32), :] + l_prec[...].astype(F32)).astype(BF)
-    to_chips(L_ALL, lambda o: l_all.at[q], l_all.at[q])
+    for j in range(2):
+        cols = pl.ds(256 * j, 256)
+        ndown[:, cols] = down[own, cols] - rate_down * (d_c[c * 2 + j].astype(F32) / total)
+        ndown_p[:, cols] = down_p[:, cols] - rate_down * (d_c[oc * 2 + j].astype(F32) / total)
+    l_all[q] = (
+        dot(ndown[...].astype(BF), dec[...], 1, 1) + dot(ndown_p[...].astype(BF), dec_p[...], 1, 1)
+    ).astype(BF)
+    each(NC, chip, L_ALL, lambda o: l_all.at[q], l_all.at[q])
+
+    @pl.when(x == c)
+    def _():
+        nd_out[...] = two_rows(ndown, z // 4, 2 * (z % 4))
+        nd_send[...] = jnp.concatenate([two_rows(ndown_p, z // 4, 2 * (z % 4))] * 4, axis=0)
+        remote(nd_send, nd_prec, ND_PAIR, pair).start()
 
     far_wait(U_B, u_b)
-    u_fin[c, q] = total_of(u_b).astype(BF)
-    to_chips(U_AG, lambda o: u_fin.at[c, q], u_fin.at[c, q])
+    u_fin[c, w] = total_of(u_b).astype(BF)
+    each(NW, wide, U_AG, lambda o: u_fin.at[c, w], u_fin.at[c, w])
 
     arrived(m_fin.at[c, pl.ds(0, 448)], M_AG)
     remote(m_fin.at[c], m_fin.at[c], M_PAIR2, pair).start()
     arrived(m_fin.at[oc], M_PAIR2)
     cp_m = load(m_fin, m_h, O_M)
 
-    arrived(u_fin.at[c, pl.ds(0, NC - 1)], U_AG)
+    @pl.when(x != c)
+    def _():
+        arrived(nd_prec, ND_PAIR)
+        nd_out[...] = nd_prec[0:2, :]
+
+    arrived(u_fin.at[c, pl.ds(0, NW - 1)], U_AG)
     remote(u_fin.at[c], u_fin.at[c], U_PAIR2, pair).start()
 
-    half = pl.ds(pl.multiple_of(c * 32, 32), 32)
     arrived(l_all.at[pl.ds(0, NC - 1)], L_ALL)
-    l_fin[half, :] = total_of(l_all).astype(BF)
-    remote(l_fin.at[half], l_fin.at[half], L_PAIR2, pair).start()
+    l_fin[own, :] = total_of(l_all).astype(BF)
+    remote(l_fin.at[own], l_fin.at[own], L_PAIR2, pair).start()
 
     arrived(u_fin.at[oc], U_PAIR2)
-    for i in range(2):
+    for i in range(4):
         for j in range(NC):
-            rows, cols = pl.ds(32 * i, 32), pl.ds(128 * j, 128)
-            grad = u_fin[i, j].astype(F32) / total
+            rows, cols = pl.ds(16 * i, 16), pl.ds(128 * j, 128)
+            grad = u_fin[i // 2, (i % 2) * NC + j].astype(F32) / total
             new = upt[rows, cols] - rate_up * grad
             upt[rows, cols] = new
             nupt16[rows, cols] = new.astype(BF)
@@ -346,15 +381,15 @@
     nup[...] = upt[:, pl.ds(pl.multiple_of(first // 128 * 128, 128), 128)].T
     nu_out[...] = two_rows(nup, first % 128 // 8, first % 8)
 
-    arrived(l_fin.at[half], L_PAIR2)
+    arrived(l_fin.at[own], L_PAIR2)
 
     m_part = m_fin.at[c, pl.ds(0, 448)]
     for ref, i in (
-        (u_send, U_PAIR), (u_rs.at[pl.ds(0, NC - 1)], U_RS),
-        (u_a.at[pl.ds(0, NA - 1)], U_A), (u_b.at[pl.ds(0, NB - 1)], U_B),
-        (u_fin.at[c, pl.ds(0, NC - 1)], U_AG), (u_fin.at[c], U_PAIR2), (m_send, M_PAIR),
+        (u_send, U_PAIR), (u_rs.at[pl.ds(0, NW - 1)], U_RS),
+        (u_a.at[pl.ds(0, GZ - 1)], U_A), (u_b.at[pl.ds(0, NB - 1)], U_B),
+        (u_fin.at[c, pl.ds(0, NW - 1)], U_AG), (u_fin.at[c], U_PAIR2), (m_send, M_PAIR),
         (m_rs.at[pl.ds(0, NC - 1)], M_RS), (m_part, M_AG), (m_fin.at[c], M_PAIR2),
-        (l_send, L_PAIR), (l_all.at[pl.ds(0, NC - 1)], L_ALL), (l_fin.at[half], L_PAIR2),
+        (dec, DEC_PAIR), (down.at[theirs], DOWN_PAIR), (l_all.at[pl.ds(0, NC - 1)], L_ALL), (l_fin.at[own], L_PAIR2),
     ):
         sent(ref, i)
 
@@ -362,7 +397,18 @@
     def _():
         sent(td_send.at[pl.ds(0, NO - 1)], D_A)
         sent(d_b.at[pl.ds(0, NB - 1)], D_B)
-        sent(d_a.at[pl.ds(0, NA - 1)], D_C)
+
+        @pl.when(x == c)
+        def _():
+            sent(d_a.at[pl.ds(0, NA - 1)], D_C)
+
+        @pl.when(x != c)
+        def _():
+            sent(d_a, D_C)
+
+    @pl.when(x == c)
+    def _():
+        sent(nd_send, ND_PAIR)
 
     @pl.when(jnp.logical_not(owner))
     def _():
@@ -408,16 +454,16 @@
         out_specs=(vmem,) * 5 + (any_,),
         scratch_shapes=[
             V((512, 512), BF), V((512, 1024), BF), V((512, 1024), BF), V((64, 512), F32),
-            V((512, 512), BF),
-            V((512, 64), BF), V((NO, 32, 256), BF), V((NA, 32, 256), BF), V((NB, 32, 256), BF),
-            V((NO, 32, 256), BF), V((64, 512), F32),
-            V((2, NC, 32, 128), F32), V((NC, 32, 128), BF), V((NC, 32, 128), BF),
-            V((NC, 32, 128), BF), V((NC, 32, 128), BF), V((NA, 32, 128), BF), V((NB, 32, 128), BF),
-            V((2, NC, 32, 128), BF), V((64, 1024), F32), V((128, 64), F32),
+            V((512, 512), BF), V((512, 512), BF), V((32, 512), F32),
+            V((512, 64), BF), V((64, 512), F32), V((NO, 32, 256), BF), V((NA, 32, 256), BF),
+            V((NB, 32, 256), BF), V((32, 256), BF), V((NO, 32, 256), BF), V((32, 512), F32),
+            V((32, 512), F32), V((8, 512), F32), V((8, 512), F32),
+            V((32, 512), BF), V((32, 512), BF), V((NW, 16, 128), BF), V((NW, 16, 128), BF),
+            V((GZ, 16, 128), BF), V((NB, 16, 128), BF), V((2, NW, 16, 128), BF),
+            V((64, 1024), F32), V((128, 64), F32),
             V((512, 512), BF), V((512, 512), F32), V((512, 512), BF), V((NC, 64, 512), BF),
-            V((NC, 64, 512), BF), V((2, 512, 512), BF),
-            V((64, 512), F32), V((32, 512), BF), V((32, 512), BF), V((NC, 32, 512), BF),
-            pltpu.SemaphoreType.DMA((16,)), pltpu.SemaphoreType.DMA((16,)),
+            V((NC, 64, 512), BF), V((2, 512, 512), BF), V((NC, 32, 512), BF),
+            pltpu.SemaphoreType.DMA((18,)), pltpu.SemaphoreType.DMA((18,)),
             pltpu.SemaphoreType.DMA((16, NB)),
             pltpu.SemaphoreType.DMA((7,)), pltpu.SemaphoreType.REGULAR,
         ],

time: 43.1 us -> 43.2 us (level)
  no operation moved by 1% of the time
where the time goes in v5:
time: 43.2 us; the launch traced here: 43.1 us
  Pallas kernels  42.5 us (98%)
  between operations  0.64 us (1%)
    pallas_call x1, Pallas kernels, body(): pl.pallas_call(comm_kernel, out_shape=(sds((512, 512), BF), sds((2, 512),...  41.2 us
    pallas_call x1, Pallas kernels, body(): pl.pallas_call(finish_kernel, out_shape=(sds((512, 1024), BF), sds((512,...  1.28 us

profile of v5, /device:TPU:1, one launch (start us, length us, event | category | flops | bytes accessed | tf_op | source)
XLA Modules:
  0.0 43.1 jit_solution(13839662548940262172)
XLA Ops:
  0.6 41.2 %adapter_step.1 = (bf16[512,512]{1,0:T(8,128)(2,1)S(1)}, f32[2,512]{1,0:T(2,128)S(1)}, f32[2,64]{1,0:T(2,128)S(1)}, bf16[64,1024]{1,0:T(8,128)(2,1)S(1)}, bf16[6...) custom-call(bf16[512,512]{1,0:T(8,128)(2,1)} %learn_h.1, bf16[512,1024]{1,0:T(8,128)(2,1)} %cot_h.1, ...), custom_call_target="tpu_custom_call" | custom-call | tf_op jit(solution)/shard_map/adapter_step/pallas_call | solution.py:447
  41.8 1.3 %finish.1 = (bf16[512,1024]{1,0:T(8,128)(2,1)}, bf16[512,512]{1,0:T(8,128)(2,1)}, f32[2,512]{1,0:T(2,128)}, f32[2,64]{1,0:T(2,128)}) custom-call(bf16[2,512,512]{2,1,0:T(8,128)(2,1)S(1)} %get-tuple-element.14.m_ref, bf16[64,512]{1,0:T(8,128)(2,1)S(1)} %get-tuple-element.15.ld_ref, bf16[64,1024]{1,0:T(8,128)(2,1)S(1)} %get-tuple-element.16.nut_ref, ...), custom_call_target="tpu_custom_call" | custom-call | tf_op jit(solution)/shard_map/finish/pallas_call | solution.py:480

commit v6 on v5

--- a/solution.py
+++ b/solution.py
@@ -20,12 +20,22 @@
 F32 = jnp.float32
 
 (D_A, D_B, D_C, U_PAIR, U_RS, U_A, U_B, U_AG, U_PAIR2,
- M_PAIR, M_RS, M_AG, M_PAIR2, DEC_PAIR, L_ALL, L_PAIR2, DOWN_PAIR, ND_PAIR) = range(18)
+ M_PAIR, M_RS, M_AG, M_PAIR2, DEC_PAIR, L_ALL, L_PAIR2, DOWN_PAIR, ND_PAIR,
+ D_A2, D_B2, D_C2) = range(21)
+DA, DB, DC = (D_A, D_A2), (D_B, D_B2), (D_C, D_C2)
 (I_COT, I_UP, I_LEARN, I_DOWN, I_DEC, I_BASE, O_M) = range(7)
 
 
 def dot(a, b, ca, cb):
     return lax.dot_general(a, b, (((ca,), (cb,)), ((), ())), preferred_element_type=F32)
+
+
+def div(a, b):
+    return lax.div(a, jnp.int32(b))
+
+
+def rem(a, b):
+    return lax.rem(a, jnp.int32(b))
 
 
 def comm_kernel(
@@ -39,13 +49,13 @@
 ):
     d = lax.axis_index("dp")
     t = lax.axis_index("tensor")
-    x = d // NZ
-    z = d % NZ
-    zb = z // GZ
-    za = z % GZ
+    x = div(d, NZ)
+    z = rem(d, NZ)
+    zb = div(z, GZ)
+    za = rem(z, GZ)
     a = x * GZ + za
-    q = t // 2
-    c = t % 2
+    q = div(t, 2)
+    c = rem(t, 2)
     oc = 1 - c
     w = x * NC + q
     total = 16384.0
@@ -62,39 +72,43 @@
     cp_dec = load(dec_h, dec, I_DEC)
     cp_base = load(base_h, base, I_BASE)
 
-    owner = jnp.logical_or(za == 1, za == 2)
-    mine = x * 2 + jnp.where(zb < 2, za - 1, 2 - za)
+    def first_owner(group):
+        return jnp.where(group == 0, 0, 1)
+
+    part = za - first_owner(zb)
+    owner = jnp.logical_or(part == 0, part == 1)
+    mine = x * 2 + part
 
     def near(k):
-        other = (a + k) % NA
-        return other, {"dp": (other // GZ) * NZ + zb * GZ + other % GZ, "tensor": t}
+        other = rem(a + k, NA)
+        return other, {"dp": div(other, GZ) * NZ + zb * GZ + rem(other, GZ), "tensor": t}
 
     def near_core(k, core):
         return {"dp": near(k)[1]["dp"], "tensor": q * 2 + core}
 
     def owner_of(o):
-        at = jnp.where(zb < 2, 1 + o % 2, 2 - o % 2)
+        at = first_owner(zb) + o % 2
         return (o // 2) * GZ + at, {"dp": (o // 2) * NZ + zb * GZ + at, "tensor": t}
 
     def column(group, at):
         return {"dp": x * NZ + group * GZ + at, "tensor": t}
 
     def far_down(k):
-        return column(k, jnp.where((zb < 2) == (k < 2), za, GZ - 1 - za))
+        return column(k, first_owner(k) + part)
 
     def far_up(k):
         opposite = jnp.logical_or(zb == k + 2, zb == k - 2)
         return column(k, jnp.where(opposite, GZ - 1 - za, za))
 
     def wide(k):
-        other = (w + k) % NW
-        return other, {"dp": (other // NC) * NZ + z, "tensor": (other % NC) * 2 + c}
+        other = rem(w + k, NW)
+        return other, {"dp": div(other, NC) * NZ + z, "tensor": rem(other, NC) * 2 + c}
 
     def above(k):
-        return {"dp": x * NZ + zb * GZ + (za + k) % GZ, "tensor": t}
+        return {"dp": x * NZ + zb * GZ + rem(za + k, GZ), "tensor": t}
 
     def chip(k):
-        other = (q + k) % NC
+        other = rem(q + k, NC)
         return other, {"dp": d, "tensor": other * 2 + c}
 
     pair = {"dp": d, "tensor": q * 2 + oc}
@@ -113,14 +127,19 @@
         greet(wide(k)[1])
         return 0
 
-    lax.fori_loop(1, NA, hello_near, 0)
-    lax.fori_loop(1, NW, hello_wide, 0)
+    for k in range(1, NA):
+        hello_near(k, 0)
+    for k in range(1, NW):
+        hello_wide(k, 0)
     greet(pair)
     for k in range(1, NB):
         @pl.when(zb < k)
         def _():
-            greet(column(k, za))
-            greet(column(k, GZ - 1 - za))
+            greet(far_up(k))
+
+        @pl.when(jnp.logical_and(zb < k, owner))
+        def _():
+            greet(far_down(k))
 
     def remote(src, dst, i, dev):
         return pltpu.make_async_remote_copy(
@@ -139,7 +158,8 @@
             other, dev = place(k)
             remote(src(other), dst, i, dev).start()
             return 0
-        lax.fori_loop(1, n, step, 0)
+        for k in range(1, n):
+            step(k, 0)
 
     def send_far(i, dev, buf, k):
         pltpu.make_async_remote_copy(
@@ -155,7 +175,7 @@
 
     def far_send(i, dev, buf, wanted):
         for step in (1, 3, 2):
-            k = (zb + step) % NB
+            k = rem(zb + step, NB)
 
             @pl.when(k > zb if wanted == "higher" else k < zb)
             def _():
@@ -163,7 +183,7 @@
 
     def far_wait(i, buf):
         for step in range(1, NB):
-            far_arrived(i, buf, (zb + step) % NB)
+            far_arrived(i, buf, rem(zb + step, NB))
 
     def total_of(ref):
         acc = ref[0].astype(F32)
@@ -191,33 +211,39 @@
     term = dot(lowout[...], learn[...], 0, 0).astype(BF)
     for k in range(NO):
         i, j = k // 2, k % 2
-        td_send[k] = term[32 * i:32 * i + 32, 256 * j:256 * j + 256]
-
-    pl.semaphore_wait(barrier, 2 * (NA - 1) + (NW - 1) + 1 + 2 * zb)
+        for h in range(2):
+            td_send[h, k] = term[32 * i:32 * i + 32, 256 * j + 128 * h:256 * j + 128 * h + 128]
+
+    far_greets = 1 + owner.astype(jnp.int32)
+    pl.semaphore_wait(barrier, 2 * (NA - 1) + (NW - 1) + 1 + far_greets * zb)
 
     remote(u_send, u_prec, U_PAIR, pair).start()
 
-    def to_owner(o, _):
-        place, dev = owner_of(o)
-
-        @pl.when(place != a)
-        def _():
-            remote(td_send.at[o], d_a.at[a], D_A, dev).start()
-        return 0
-
-    lax.fori_loop(0, NO, to_owner, 0)
+    for h in range(2):
+        for o in range(NO):
+            place, dev = owner_of(o)
+
+            @pl.when(place != a)
+            def _():
+                remote(td_send.at[h, o], d_a.at[h, a], DA[h], dev).start()
 
     for k in range(NB - 1):
         @pl.when(k < zb)
         def _():
-            for at in (za, GZ - 1 - za):
-                pl.semaphore_signal(
-                    entered, inc=1, device_id=column(k, at), device_id_type=pl.DeviceIdType.MESH
-                )
+            pl.semaphore_signal(
+                entered, inc=1, device_id=far_up(k), device_id_type=pl.DeviceIdType.MESH
+            )
+
+        @pl.when(jnp.logical_and(k < zb, owner))
+        def _():
+            pl.semaphore_signal(
+                entered, inc=1, device_id=far_down(k), device_id_type=pl.DeviceIdType.MESH
+            )
 
     @pl.when(owner)
     def _():
-        d_a[a] = td_send[mine]
+        for h in range(2):
+            d_a[h, a] = td_send[h, mine]
 
     cp_dec.wait()
     cp_base.wait()
@@ -264,9 +290,10 @@
 
     @pl.when(owner)
     def _():
-        arrived(d_a.at[pl.ds(0, NA - 1)], D_A)
-        d_b[zb] = total_of(d_a).astype(BF)
-        far_send(D_B, far_down, d_b, "lower")
+        for h in range(2):
+            arrived(d_a.at[h, pl.ds(0, NA - 1)], DA[h])
+            d_b[h, zb] = total_of(d_a.at[h]).astype(BF)
+            far_send(DB[h], far_down, d_b.at[h], "lower")
 
     arrived(u_rs.at[pl.ds(0, NW - 1)], U_RS)
     u_a[za] = total_of(u_rs).astype(BF)
@@ -284,11 +311,12 @@
 
     @pl.when(zb < NB - 1)
     def _():
-        pl.semaphore_wait(entered, 2 * (NB - 1 - zb))
+        pl.semaphore_wait(entered, far_greets * (NB - 1 - zb))
 
     @pl.when(owner)
     def _():
-        far_send(D_B, far_down, d_b, "higher")
+        for h in range(2):
+            far_send(DB[h], far_down, d_b.at[h], "higher")
 
     far_send(U_B, far_up, u_b, "higher")
 
@@ -303,40 +331,38 @@
 
     @pl.when(owner)
     def _():
-        far_wait(D_B, d_b)
-        d_o[...] = total_of(d_b).astype(BF)
-        slot = c * 2 + mine % 2
-
-        def to_core(k, _):
-            remote(d_o, d_c.at[slot], D_C, near_core(k, x)).start()
-            return 0
-
-        lax.fori_loop(1, NA, to_core, 0)
-
-        @pl.when(x == c)
-        def _():
-            d_c[slot] = d_o[...]
-
-        @pl.when(x != c)
-        def _():
-            remote(d_o, d_c.at[slot], D_C, pair).start()
+        slot = c * 2 + part
+        for h in range(2):
+            far_wait(DB[h], d_b.at[h])
+            d_o[h] = total_of(d_b.at[h]).astype(BF)
+            for k in range(1, NA):
+                remote(d_o.at[h], d_c.at[h, slot], DC[h], near_core(k, x)).start()
+
+            @pl.when(x == c)
+            def _():
+                d_c[h, slot] = d_o[h]
+
+            @pl.when(x != c)
+            def _():
+                remote(d_o.at[h], d_c.at[h, slot], DC[h], pair).start()
 
     arrived(dec_p, DEC_PAIR)
     arrived(down_p, DOWN_PAIR)
     holds = jnp.logical_and(owner, x == c)
 
-    @pl.when(holds)
-    def _():
-        arrived(d_c.at[pl.ds(0, NO - 1)], D_C)
-
-    @pl.when(jnp.logical_not(holds))
-    def _():
-        arrived(d_c, D_C)
-
-    for j in range(2):
-        cols = pl.ds(256 * j, 256)
-        ndown[:, cols] = down[own, cols] - rate_down * (d_c[c * 2 + j].astype(F32) / total)
-        ndown_p[:, cols] = down_p[:, cols] - rate_down * (d_c[oc * 2 + j].astype(F32) / total)
+    for h in range(2):
+        @pl.when(holds)
+        def _():
+            arrived(d_c.at[h, pl.ds(0, NO - 1)], DC[h])
+
+        @pl.when(jnp.logical_not(holds))
+        def _():
+            arrived(d_c.at[h], DC[h])
+
+        for j in range(2):
+            cols = pl.ds(256 * j + 128 * h, 128)
+            ndown[:, cols] = down[own, cols] - rate_down * (d_c[h, c * 2 + j].astype(F32) / total)
+            ndown_p[:, cols] = down_p[:, cols] - rate_down * (d_c[h, oc * 2 + j].astype(F32) / total)
     l_all[q] = (
         dot(ndown[...].astype(BF), dec[...], 1, 1) + dot(ndown_p[...].astype(BF), dec_p[...], 1, 1)
     ).astype(BF)
@@ -344,8 +370,8 @@
 
     @pl.when(x == c)
     def _():
-        nd_out[...] = two_rows(ndown, z // 4, 2 * (z % 4))
-        nd_send[...] = jnp.concatenate([two_rows(ndown_p, z // 4, 2 * (z % 4))] * 4, axis=0)
+        nd_out[...] = two_rows(ndown, div(z, 4), 2 * rem(z, 4))
+        nd_send[...] = jnp.concatenate([two_rows(ndown_p, div(z, 4), 2 * rem(z, 4))] * 4, axis=0)
         remote(nd_send, nd_prec, ND_PAIR, pair).start()
 
     far_wait(U_B, u_b)
@@ -378,8 +404,8 @@
             upt[rows, cols] = new
             nupt16[rows, cols] = new.astype(BF)
     first = d * 32 + t * 2
-    nup[...] = upt[:, pl.ds(pl.multiple_of(first // 128 * 128, 128), 128)].T
-    nu_out[...] = two_rows(nup, first % 128 // 8, first % 8)
+    nup[...] = upt[:, pl.ds(pl.multiple_of(div(first, 128) * 128, 128), 128)].T
+    nu_out[...] = two_rows(nup, div(rem(first, 128), 8), rem(first, 8))
 
     arrived(l_fin.at[own], L_PAIR2)
 
@@ -393,26 +419,28 @@
     ):
         sent(ref, i)
 
-    @pl.when(owner)
-    def _():
-        sent(td_send.at[pl.ds(0, NO - 1)], D_A)
-        sent(d_b.at[pl.ds(0, NB - 1)], D_B)
-
-        @pl.when(x == c)
-        def _():
-            sent(d_a.at[pl.ds(0, NA - 1)], D_C)
-
-        @pl.when(x != c)
-        def _():
-            sent(d_a, D_C)
+    for h in range(2):
+        @pl.when(owner)
+        def _():
+            sent(td_send.at[h, pl.ds(0, NO - 1)], DA[h])
+            sent(d_b.at[h, pl.ds(0, NB - 1)], DB[h])
+
+            @pl.when(x == c)
+            def _():
+                sent(d_a.at[h, pl.ds(0, NA - 1)], DC[h])
+
+            @pl.when(x != c)
+            def _():
+                sent(d_a.at[h], DC[h])
+
+        @pl.when(jnp.logical_not(owner))
+        def _():
+            sent(td_send.at[h], DA[h])
 
     @pl.when(x == c)
     def _():
         sent(nd_send, ND_PAIR)
 
-    @pl.when(jnp.logical_not(owner))
-    def _():
-        sent(td_send, D_A)
 
     cp_m.wait()
 
@@ -455,16 +483,16 @@
         scratch_shapes=[
             V((512, 512), BF), V((512, 1024), BF), V((512, 1024), BF), V((64, 512), F32),
             V((512, 512), BF), V((512, 512), BF), V((32, 512), F32),
-            V((512, 64), BF), V((64, 512), F32), V((NO, 32, 256), BF), V((NA, 32, 256), BF),
-            V((NB, 32, 256), BF), V((32, 256), BF), V((NO, 32, 256), BF), V((32, 512), F32),
+            V((512, 64), BF), V((64, 512), F32), V((2, NO, 32, 128), BF), V((2, NA, 32, 128), BF),
+            V((2, NB, 32, 128), BF), V((2, 32, 128), BF), V((2, NO, 32, 128), BF), V((32, 512), F32),
             V((32, 512), F32), V((8, 512), F32), V((8, 512), F32),
             V((32, 512), BF), V((32, 512), BF), V((NW, 16, 128), BF), V((NW, 16, 128), BF),
             V((GZ, 16, 128), BF), V((NB, 16, 128), BF), V((2, NW, 16, 128), BF),
             V((64, 1024), F32), V((128, 64), F32),
             V((512, 512), BF), V((512, 512), F32), V((512, 512), BF), V((NC, 64, 512), BF),
             V((NC, 64, 512), BF), V((2, 512, 512), BF), V((NC, 32, 512), BF),
-            pltpu.SemaphoreType.DMA((18,)), pltpu.SemaphoreType.DMA((18,)),
-            pltpu.SemaphoreType.DMA((16, NB)),
+            pltpu.SemaphoreType.DMA((21,)), pltpu.SemaphoreType.DMA((21,)),
+            pltpu.SemaphoreType.DMA((21, NB)),
             pltpu.SemaphoreType.DMA((7,)), pltpu.SemaphoreType.REGULAR,
         ],
         compiler_params=pltpu.CompilerParams(

time: 43.2 us -> 41.9 us (0.970)
  Pallas kernels: 42.5 us -> 41.1 us
    pallas_call x1, Pallas kernels: 41.2 us -> 39.8 us  [body(): pl.pallas_call(comm_kernel, out_shape=(sds((512, 512), BF), sds((2, 512),...]
where the time goes in v6:
time: 41.9 us; the launch traced here: 41.7 us
  Pallas kernels  41.1 us (98%)
  between operations  0.64 us (2%)
    pallas_call x1, Pallas kernels, body(): pl.pallas_call(comm_kernel, out_shape=(sds((512, 512), BF), sds((2, 512),...  39.8 us
    pallas_call x1, Pallas kernels, body(): pl.pallas_call(finish_kernel, out_shape=(sds((512, 1024), BF), sds((512,...  1.29 us

profile of v6, /device:TPU:1, one launch (start us, length us, event | category | flops | bytes accessed | tf_op | source)
XLA Modules:
  0.0 41.7 jit_solution(14107512978561101463)
XLA Ops:
  0.6 39.8 %adapter_step.1 = (bf16[512,512]{1,0:T(8,128)(2,1)S(1)}, f32[2,512]{1,0:T(2,128)S(1)}, f32[2,64]{1,0:T(2,128)S(1)}, bf16[64,1024]{1,0:T(8,128)(2,1)S(1)}, bf16[6...) custom-call(bf16[512,512]{1,0:T(8,128)(2,1)} %learn_h.1, bf16[512,1024]{1,0:T(8,128)(2,1)} %cot_h.1, ...), custom_call_target="tpu_custom_call" | custom-call | tf_op jit(solution)/shard_map/adapter_step/pallas_call | solution.py:475
  40.4 1.3 %finish.1 = (bf16[512,1024]{1,0:T(8,128)(2,1)}, bf16[512,512]{1,0:T(8,128)(2,1)}, f32[2,512]{1,0:T(2,128)}, f32[2,64]{1,0:T(2,128)}) custom-call(bf16[2,512,512]{2,1,0:T(8,128)(2,1)S(1)} %get-tuple-element.14.m_ref, bf16[64,512]{1,0:T(8,128)(2,1)S(1)} %get-tuple-element.15.ld_ref, bf16[64,1024]{1,0:T(8,128)(2,1)S(1)} %get-tuple-element.16.nut_ref, ...), custom_call_target="tpu_custom_call" | custom-call | tf_op jit(solution)/shard_map/finish/pallas_call | solution.py:508

commit v7 on v6

--- a/solution.py
+++ b/solution.py
@@ -16,12 +16,16 @@
 NC = 8
 NW = 16
 
+FAR_NEAR = (2, 6, 3, 5, 1, 7, 4)
+FAR_CHIP = (3, 5, 1, 7, 4, 2, 6)
+FAR_WIDE = (3, 13, 5, 11, 4, 12, 1, 15, 6, 10, 7, 9, 2, 14, 8)
+
 BF = jnp.bfloat16
 F32 = jnp.float32
 
 (D_A, D_B, D_C, U_PAIR, U_RS, U_A, U_B, U_AG, U_PAIR2,
- M_PAIR, M_RS, M_AG, M_PAIR2, DEC_PAIR, L_ALL, L_PAIR2, DOWN_PAIR, ND_PAIR,
- D_A2, D_B2, D_C2) = range(21)
+ M_PAIR, M_RS, M_AG, M_PAIR2, DEC_PAIR, L_Y0, L_PAIR2, DOWN_PAIR, ND_PAIR,
+ D_A2, D_B2, D_C2, L_X0, L_X1, L_Y1) = range(24)
 DA, DB, DC = (D_A, D_A2), (D_B, D_B2), (D_C, D_C2)
 (I_COT, I_UP, I_LEARN, I_DOWN, I_DEC, I_BASE, O_M) = range(7)
 
@@ -44,7 +48,7 @@
     learn, cot, base, down, dec, dec_p, down_p,
     lowout, low_in, td_send, d_a, d_b, d_o, d_c, ndown, ndown_p, nd_send, nd_prec,
     u_send, u_prec, u_sum, u_rs, u_a, u_b, u_fin, upt, nup,
-    m_send, m_keep, m_prec, m_sum, m_rs, m_fin, l_all,
+    m_send, m_keep, m_prec, m_sum, m_rs, m_fin, l_y0, l_x0, l_x1, l_y1,
     ssem, rsem, rfar, lsem, entered,
 ):
     d = lax.axis_index("dp")
@@ -57,6 +61,8 @@
     q = div(t, 2)
     c = rem(t, 2)
     oc = 1 - c
+    yy = div(q, 2)
+    xh = rem(q, 2)
     w = x * NC + q
     total = 16384.0
 
@@ -107,6 +113,11 @@
     def above(k):
         return {"dp": x * NZ + zb * GZ + rem(za + k, GZ), "tensor": t}
 
+    def along_y(k):
+        return {"dp": d, "tensor": rem(yy + k, 4) * 4 + xh * 2 + c}
+
+    along_x = {"dp": d, "tensor": yy * 4 + (1 - xh) * 2 + c}
+
     def chip(k):
         other = rem(q + k, NC)
         return other, {"dp": d, "tensor": other * 2 + c}
@@ -127,9 +138,9 @@
         greet(wide(k)[1])
         return 0
 
-    for k in range(1, NA):
+    for k in FAR_NEAR:
         hello_near(k, 0)
-    for k in range(1, NW):
+    for k in FAR_WIDE:
         hello_wide(k, 0)
     greet(pair)
     for k in range(1, NB):
@@ -153,12 +164,12 @@
     def sent(ref, i):
         remote(ref, ref, i, pair).wait_send()
 
-    def each(n, place, i, src, dst):
+    def each(order, place, i, src, dst):
         def step(k, _):
             other, dev = place(k)
             remote(src(other), dst, i, dev).start()
             return 0
-        for k in range(1, n):
+        for k in order:
             step(k, 0)
 
     def send_far(i, dev, buf, k):
@@ -245,24 +256,6 @@
         for h in range(2):
             d_a[h, a] = td_send[h, mine]
 
-    cp_dec.wait()
-    cp_base.wait()
-
-    def other_half(r, _):
-        to = pl.ds(pl.multiple_of(r * 256, 256), 256)
-        cols = pl.ds(pl.multiple_of(oc * 512 + r * 256, 256), 256)
-        m_send[:, to] = dot(dec[...], base[:, cols], 1, 0).astype(BF)
-        return 0
-
-    def own_half(r, _):
-        to = pl.ds(pl.multiple_of(r * 256, 256), 256)
-        cols = pl.ds(pl.multiple_of(c * 512 + r * 256, 256), 256)
-        m_keep[:, to] = dot(dec[...], base[:, cols], 1, 0)
-        return 0
-
-    lax.fori_loop(0, 2, other_half, 0)
-    remote(m_send, m_prec, M_PAIR, pair).start()
-
     arrived(u_prec, U_PAIR)
     pair_in = (low_in[own, :] + u_prec[...].astype(F32)).astype(BF)
     term_up = dot(pair_in, cot[...], 1, 0).astype(BF)
@@ -270,12 +263,37 @@
         for j in range(NC):
             u_sum[i * NC + j] = term_up[16 * i:16 * i + 16, 128 * j:128 * j + 128]
     u_rs[w] = u_sum[w]
-    each(NW, wide, U_RS, lambda o: u_sum.at[o], u_rs.at[w])
+    each(FAR_WIDE, wide, U_RS, lambda o: u_sum.at[o], u_rs.at[w])
+
+    cp_dec.wait()
+    cp_base.wait()
+
+    def other_half(r, _):
+        to = pl.ds(pl.multiple_of(r * 256, 256), 256)
+        cols = pl.ds(pl.multiple_of(oc * 512 + r * 256, 256), 256)
+        m_send[:, to] = dot(dec[...], base[:, cols], 1, 0).astype(BF)
+        return 0
+
+    def own_half(r, _):
+        to = pl.ds(pl.multiple_of(r * 256, 256), 256)
+        cols = pl.ds(pl.multiple_of(c * 512 + r * 256, 256), 256)
+        m_keep[:, to] = dot(dec[...], base[:, cols], 1, 0)
+        return 0
+
+    lax.fori_loop(0, 2, other_half, 0)
+    remote(m_send, m_prec, M_PAIR, pair).start()
 
     remote(dec, dec_p, DEC_PAIR, pair).start()
     remote(down.at[theirs], down_p, DOWN_PAIR, pair).start()
 
     lax.fori_loop(0, 2, own_half, 0)
+    @pl.when(owner)
+    def _():
+        for h in range(2):
+            arrived(d_a.at[h, pl.ds(0, NA - 1)], DA[h])
+            d_b[h, zb] = total_of(d_a.at[h]).astype(BF)
+            far_send(DB[h], far_down, d_b.at[h], "lower")
+
     arrived(m_prec, M_PAIR)
 
     def add_half(r, _):
@@ -286,14 +304,7 @@
     lax.fori_loop(0, NC, add_half, 0)
     m_rs[q] = m_sum[q]
 
-    each(NC, chip, M_RS, lambda o: m_sum.at[o], m_rs.at[q])
-
-    @pl.when(owner)
-    def _():
-        for h in range(2):
-            arrived(d_a.at[h, pl.ds(0, NA - 1)], DA[h])
-            d_b[h, zb] = total_of(d_a.at[h]).astype(BF)
-            far_send(DB[h], far_down, d_b.at[h], "lower")
+    each(FAR_CHIP, chip, M_RS, lambda o: m_sum.at[o], m_rs.at[q])
 
     arrived(u_rs.at[pl.ds(0, NW - 1)], U_RS)
     u_a[za] = total_of(u_rs).astype(BF)
@@ -307,7 +318,7 @@
     my_rows = pl.ds(pl.multiple_of(q * 64, 64), 64)
     arrived(m_rs.at[pl.ds(0, NC - 1)], M_RS)
     m_fin[c, my_rows, :] = total_of(m_rs).astype(BF)
-    each(NC, chip, M_AG, lambda o: m_fin.at[c, my_rows], m_fin.at[c, my_rows])
+    each(FAR_CHIP, chip, M_AG, lambda o: m_fin.at[c, my_rows], m_fin.at[c, my_rows])
 
     @pl.when(zb < NB - 1)
     def _():
@@ -335,7 +346,7 @@
         for h in range(2):
             far_wait(DB[h], d_b.at[h])
             d_o[h] = total_of(d_b.at[h]).astype(BF)
-            for k in range(1, NA):
+            for k in FAR_NEAR:
                 remote(d_o.at[h], d_c.at[h, slot], DC[h], near_core(k, x)).start()
 
             @pl.when(x == c)
@@ -363,10 +374,14 @@
             cols = pl.ds(256 * j + 128 * h, 128)
             ndown[:, cols] = down[own, cols] - rate_down * (d_c[h, c * 2 + j].astype(F32) / total)
             ndown_p[:, cols] = down_p[:, cols] - rate_down * (d_c[h, oc * 2 + j].astype(F32) / total)
-    l_all[q] = (
+    low = (
         dot(ndown[...].astype(BF), dec[...], 1, 1) + dot(ndown_p[...].astype(BF), dec_p[...], 1, 1)
     ).astype(BF)
-    each(NC, chip, L_ALL, lambda o: l_all.at[q], l_all.at[q])
+    l_y0[yy] = low[:, :256]
+    for k in (2, 1, 3):
+        remote(l_y0.at[yy], l_y0.at[yy], L_Y0, along_y(k)).start()
+    l_x1[xh] = low[:, 256:]
+    remote(l_x1.at[xh], l_x1.at[xh], L_X1, along_x).start()
 
     @pl.when(x == c)
     def _():
@@ -376,10 +391,18 @@
 
     far_wait(U_B, u_b)
     u_fin[c, w] = total_of(u_b).astype(BF)
-    each(NW, wide, U_AG, lambda o: u_fin.at[c, w], u_fin.at[c, w])
+    each(FAR_WIDE, wide, U_AG, lambda o: u_fin.at[c, w], u_fin.at[c, w])
 
     arrived(m_fin.at[c, pl.ds(0, 448)], M_AG)
     remote(m_fin.at[c], m_fin.at[c], M_PAIR2, pair).start()
+    arrived(l_x1.at[0], L_X1)
+    l_y1[yy] = total_of(l_x1).astype(BF)
+    for k in (2, 1, 3):
+        remote(l_y1.at[yy], l_y1.at[yy], L_Y1, along_y(k)).start()
+    arrived(l_y0.at[pl.ds(0, 3)], L_Y0)
+    l_x0[xh] = total_of(l_y0).astype(BF)
+    remote(l_x0.at[xh], l_x0.at[xh], L_X0, along_x).start()
+
     arrived(m_fin.at[oc], M_PAIR2)
     cp_m = load(m_fin, m_h, O_M)
 
@@ -391,8 +414,10 @@
     arrived(u_fin.at[c, pl.ds(0, NW - 1)], U_AG)
     remote(u_fin.at[c], u_fin.at[c], U_PAIR2, pair).start()
 
-    arrived(l_all.at[pl.ds(0, NC - 1)], L_ALL)
-    l_fin[own, :] = total_of(l_all).astype(BF)
+    arrived(l_x0.at[0], L_X0)
+    l_fin[own, :256] = total_of(l_x0).astype(BF)
+    arrived(l_y1.at[pl.ds(0, 3)], L_Y1)
+    l_fin[own, 256:] = total_of(l_y1).astype(BF)
     remote(l_fin.at[own], l_fin.at[own], L_PAIR2, pair).start()
 
     arrived(u_fin.at[oc], U_PAIR2)
@@ -415,7 +440,8 @@
         (u_a.at[pl.ds(0, GZ - 1)], U_A), (u_b.at[pl.ds(0, NB - 1)], U_B),
         (u_fin.at[c, pl.ds(0, NW - 1)], U_AG), (u_fin.at[c], U_PAIR2), (m_send, M_PAIR),
         (m_rs.at[pl.ds(0, NC - 1)], M_RS), (m_part, M_AG), (m_fin.at[c], M_PAIR2),
-        (dec, DEC_PAIR), (down.at[theirs], DOWN_PAIR), (l_all.at[pl.ds(0, NC - 1)], L_ALL), (l_fin.at[own], L_PAIR2),
+        (dec, DEC_PAIR), (down.at[theirs], DOWN_PAIR), (l_y0.at[pl.ds(0, 3)], L_Y0),
+        (l_x0.at[0], L_X0), (l_x1.at[0], L_X1), (l_y1.at[pl.ds(0, 3)], L_Y1), (l_fin.at[own], L_PAIR2),
     ):
         sent(ref, i)
 
@@ -490,8 +516,9 @@
             V((GZ, 16, 128), BF), V((NB, 16, 128), BF), V((2, NW, 16, 128), BF),
             V((64, 1024), F32), V((128, 64), F32),
             V((512, 512), BF), V((512, 512), F32), V((512, 512), BF), V((NC, 64, 512), BF),
-            V((NC, 64, 512), BF), V((2, 512, 512), BF), V((NC, 32, 512), BF),
-            pltpu.SemaphoreType.DMA((21,)), pltpu.SemaphoreType.DMA((21,)),
+            V((NC, 64, 512), BF), V((2, 512, 512), BF), V((4, 32, 256), BF),
+            V((2, 32, 256), BF), V((2, 32, 256), BF), V((4, 32, 256), BF),
+            pltpu.SemaphoreType.DMA((24,)), pltpu.SemaphoreType.DMA((24,)),
             pltpu.SemaphoreType.DMA((21, NB)),
             pltpu.SemaphoreType.DMA((7,)), pltpu.SemaphoreType.REGULAR,
         ],

time: 41.9 us -> 41.1 us (0.981)
  Pallas kernels: 41.1 us -> 40.3 us
    pallas_call x1, Pallas kernels: 39.8 us -> 39 us  [body(): pl.pallas_call(comm_kernel, out_shape=(sds((512, 512), BF), sds((2, 512),...]
where the time goes in v7:
time: 41.1 us; the launch traced here: 40.9 us
  Pallas kernels  40.3 us (98%)
  between operations  0.64 us (2%)
    pallas_call x1, Pallas kernels, body(): pl.pallas_call(comm_kernel, out_shape=(sds((512, 512), BF), sds((2, 512),...  39 us
    pallas_call x1, Pallas kernels, body(): pl.pallas_call(finish_kernel, out_shape=(sds((512, 1024), BF), sds((512,...  1.28 us

profile of v7, /device:TPU:1, one launch (start us, length us, event | category | flops | bytes accessed | tf_op | source)
XLA Modules:
  0.0 40.9 jit_solution(127854673175364414)
XLA Ops:
  0.6 39.0 %adapter_step.1 = (bf16[512,512]{1,0:T(8,128)(2,1)S(1)}, f32[2,512]{1,0:T(2,128)S(1)}, f32[2,64]{1,0:T(2,128)S(1)}, bf16[64,1024]{1,0:T(8,128)(2,1)S(1)}, bf16[6...) custom-call(bf16[512,512]{1,0:T(8,128)(2,1)} %learn_h.1, bf16[512,1024]{1,0:T(8,128)(2,1)} %cot_h.1, ...), custom_call_target="tpu_custom_call" | custom-call | tf_op jit(solution)/shard_map/adapter_step/pallas_call | solution.py:501
  39.7 1.3 %finish.1 = (bf16[512,1024]{1,0:T(8,128)(2,1)}, bf16[512,512]{1,0:T(8,128)(2,1)}, f32[2,512]{1,0:T(2,128)}, f32[2,64]{1,0:T(2,128)}) custom-call(bf16[2,512,512]{2,1,0:T(8,128)(2,1)S(1)} %get-tuple-element.14.m_ref, bf16[64,512]{1,0:T(8,128)(2,1)S(1)} %get-tuple-element.15.ld_ref, bf16[64,1024]{1,0:T(8,128)(2,1)S(1)} %get-tuple-element.16.nut_ref, ...), custom_call_target="tpu_custom_call" | custom-call | tf_op jit(solution)/shard_map/finish/pallas_call | solution.py:535

commit v8 on v7

--- a/solution.py
+++ b/solution.py
@@ -17,6 +17,7 @@
 NW = 16
 
 FAR_NEAR = (2, 6, 3, 5, 1, 7, 4)
+BELOW_FIRST = (7, 3, 2, 6, 5, 1, 4)
 FAR_CHIP = (3, 5, 1, 7, 4, 2, 6)
 FAR_WIDE = (3, 13, 5, 11, 4, 12, 1, 15, 6, 10, 7, 9, 2, 14, 8)
 
@@ -185,9 +186,7 @@
         ).wait_recv()
 
     def far_send(i, dev, buf, wanted):
-        for step in (1, 3, 2):
-            k = rem(zb + step, NB)
-
+        for k in range(NB):
             @pl.when(k > zb if wanted == "higher" else k < zb)
             def _():
                 send_far(i, dev, buf, k)
@@ -346,9 +345,6 @@
         for h in range(2):
             far_wait(DB[h], d_b.at[h])
             d_o[h] = total_of(d_b.at[h]).astype(BF)
-            for k in FAR_NEAR:
-                remote(d_o.at[h], d_c.at[h, slot], DC[h], near_core(k, x)).start()
-
             @pl.when(x == c)
             def _():
                 d_c[h, slot] = d_o[h]
@@ -356,6 +352,9 @@
             @pl.when(x != c)
             def _():
                 remote(d_o.at[h], d_c.at[h, slot], DC[h], pair).start()
+
+            for k in BELOW_FIRST:
+                remote(d_o.at[h], d_c.at[h, slot], DC[h], near_core(k, x)).start()
 
     arrived(dec_p, DEC_PAIR)
     arrived(down_p, DOWN_PAIR)
@@ -406,6 +405,38 @@
     arrived(m_fin.at[oc], M_PAIR2)
     cp_m = load(m_fin, m_h, O_M)
 
+    m_part = m_fin.at[c, pl.ds(0, 448)]
+    for ref, i in (
+        (u_send, U_PAIR), (u_rs.at[pl.ds(0, NW - 1)], U_RS),
+        (u_a.at[pl.ds(0, GZ - 1)], U_A), (u_b.at[pl.ds(0, NB - 1)], U_B), (m_send, M_PAIR),
+        (m_rs.at[pl.ds(0, NC - 1)], M_RS), (m_part, M_AG),
+        (dec, DEC_PAIR), (down.at[theirs], DOWN_PAIR),
+    ):
+        sent(ref, i)
+
+    for h in range(2):
+        @pl.when(owner)
+        def _():
+            sent(td_send.at[h, pl.ds(0, NO - 1)], DA[h])
+            sent(d_b.at[h, pl.ds(0, NB - 1)], DB[h])
+
+            @pl.when(x == c)
+            def _():
+                sent(d_a.at[h, pl.ds(0, NA - 1)], DC[h])
+
+            @pl.when(x != c)
+            def _():
+                sent(d_a.at[h], DC[h])
+
+        @pl.when(jnp.logical_not(owner))
+        def _():
+            sent(td_send.at[h], DA[h])
+
+    @pl.when(x == c)
+    def _():
+        sent(nd_send, ND_PAIR)
+
+
     @pl.when(x != c)
     def _():
         arrived(nd_prec, ND_PAIR)
@@ -434,40 +465,12 @@
 
     arrived(l_fin.at[own], L_PAIR2)
 
-    m_part = m_fin.at[c, pl.ds(0, 448)]
     for ref, i in (
-        (u_send, U_PAIR), (u_rs.at[pl.ds(0, NW - 1)], U_RS),
-        (u_a.at[pl.ds(0, GZ - 1)], U_A), (u_b.at[pl.ds(0, NB - 1)], U_B),
-        (u_fin.at[c, pl.ds(0, NW - 1)], U_AG), (u_fin.at[c], U_PAIR2), (m_send, M_PAIR),
-        (m_rs.at[pl.ds(0, NC - 1)], M_RS), (m_part, M_AG), (m_fin.at[c], M_PAIR2),
-        (dec, DEC_PAIR), (down.at[theirs], DOWN_PAIR), (l_y0.at[pl.ds(0, 3)], L_Y0),
-        (l_x0.at[0], L_X0), (l_x1.at[0], L_X1), (l_y1.at[pl.ds(0, 3)], L_Y1), (l_fin.at[own], L_PAIR2),
+        (u_fin.at[c, pl.ds(0, NW - 1)], U_AG), (u_fin.at[c], U_PAIR2), (m_fin.at[c], M_PAIR2),
+        (l_y0.at[pl.ds(0, 3)], L_Y0), (l_x0.at[0], L_X0), (l_x1.at[0], L_X1),
+        (l_y1.at[pl.ds(0, 3)], L_Y1), (l_fin.at[own], L_PAIR2),
     ):
         sent(ref, i)
-
-    for h in range(2):
-        @pl.when(owner)
-        def _():
-            sent(td_send.at[h, pl.ds(0, NO - 1)], DA[h])
-            sent(d_b.at[h, pl.ds(0, NB - 1)], DB[h])
-
-            @pl.when(x == c)
-            def _():
-                sent(d_a.at[h, pl.ds(0, NA - 1)], DC[h])
-
-            @pl.when(x != c)
-            def _():
-                sent(d_a.at[h], DC[h])
-
-        @pl.when(jnp.logical_not(owner))
-        def _():
-            sent(td_send.at[h], DA[h])
-
-    @pl.when(x == c)
-    def _():
-        sent(nd_send, ND_PAIR)
-
-
     cp_m.wait()
 
 

time: 41.1 us -> 40.9 us (level)
  no operation moved by 1% of the time
where the time goes in v8:
time: 40.9 us; the launch traced here: 40.8 us
  Pallas kernels  40.1 us (98%)
  between operations  0.64 us (2%)
    pallas_call x1, Pallas kernels, body(): pl.pallas_call(comm_kernel, out_shape=(sds((512, 512), BF), sds((2, 512),...  38.8 us
    pallas_call x1, Pallas kernels, body(): pl.pallas_call(finish_kernel, out_shape=(sds((512, 1024), BF), sds((512,...  1.28 us

profile of v8, /device:TPU:1, one launch (start us, length us, event | category | flops | bytes accessed | tf_op | source)
XLA Modules:
  0.0 40.8 jit_solution(1765996933089456282)
XLA Ops:
  0.6 38.8 %adapter_step.1 = (bf16[512,512]{1,0:T(8,128)(2,1)S(1)}, f32[2,512]{1,0:T(2,128)S(1)}, f32[2,64]{1,0:T(2,128)S(1)}, bf16[64,1024]{1,0:T(8,128)(2,1)S(1)}, bf16[6...) custom-call(bf16[512,512]{1,0:T(8,128)(2,1)} %learn_h.1, bf16[512,1024]{1,0:T(8,128)(2,1)} %cot_h.1, ...), custom_call_target="tpu_custom_call" | custom-call | tf_op jit(solution)/shard_map/adapter_step/pallas_call | solution.py:504
  39.5 1.3 %finish.1 = (bf16[512,1024]{1,0:T(8,128)(2,1)}, bf16[512,512]{1,0:T(8,128)(2,1)}, f32[2,512]{1,0:T(2,128)}, f32[2,64]{1,0:T(2,128)}) custom-call(bf16[2,512,512]{2,1,0:T(8,128)(2,1)S(1)} %get-tuple-element.14.m_ref, bf16[64,512]{1,0:T(8,128)(2,1)S(1)} %get-tuple-element.15.ld_ref, bf16[64,1024]{1,0:T(8,128)(2,1)S(1)} %get-tuple-element.16.nut_ref, ...), custom_call_target="tpu_custom_call" | custom-call | tf_op jit(solution)/shard_map/finish/pallas_call | solution.py:538

commit v9 on v8

--- a/solution.py
+++ b/solution.py
@@ -360,6 +360,7 @@
     arrived(down_p, DOWN_PAIR)
     holds = jnp.logical_and(owner, x == c)
 
+    low = jnp.zeros((32, 512), F32)
     for h in range(2):
         @pl.when(holds)
         def _():
@@ -373,9 +374,9 @@
             cols = pl.ds(256 * j + 128 * h, 128)
             ndown[:, cols] = down[own, cols] - rate_down * (d_c[h, c * 2 + j].astype(F32) / total)
             ndown_p[:, cols] = down_p[:, cols] - rate_down * (d_c[h, oc * 2 + j].astype(F32) / total)
-    low = (
-        dot(ndown[...].astype(BF), dec[...], 1, 1) + dot(ndown_p[...].astype(BF), dec_p[...], 1, 1)
-    ).astype(BF)
+            low += dot(ndown[:, cols].astype(BF), dec[:, cols], 1, 1)
+            low += dot(ndown_p[:, cols].astype(BF), dec_p[:, cols], 1, 1)
+    low = low.astype(BF)
     l_y0[yy] = low[:, :256]
     for k in (2, 1, 3):
         remote(l_y0.at[yy], l_y0.at[yy], L_Y0, along_y(k)).start()

time: 40.9 us -> 40.7 us (level)
  no operation moved by 1% of the time
where the time goes in v9:
time: 40.7 us; the launch traced here: 40.5 us
  Pallas kernels  39.9 us (98%)
  between operations  0.64 us (2%)
    pallas_call x1, Pallas kernels, body(): pl.pallas_call(comm_kernel, out_shape=(sds((512, 512), BF), sds((2, 512),...  38.6 us
    pallas_call x1, Pallas kernels, body(): pl.pallas_call(finish_kernel, out_shape=(sds((512, 1024), BF), sds((512,...  1.29 us

profile of v9, /device:TPU:1, one launch (start us, length us, event | category | flops | bytes accessed | tf_op | source)
XLA Modules:
  0.0 40.5 jit_solution(2844543970513040777)
XLA Ops:
  0.6 38.6 %adapter_step.1 = (bf16[512,512]{1,0:T(8,128)(2,1)S(1)}, f32[2,512]{1,0:T(2,128)S(1)}, f32[2,64]{1,0:T(2,128)S(1)}, bf16[64,1024]{1,0:T(8,128)(2,1)S(1)}, bf16[6...) custom-call(bf16[512,512]{1,0:T(8,128)(2,1)} %learn_h.1, bf16[512,1024]{1,0:T(8,128)(2,1)} %cot_h.1, ...), custom_call_target="tpu_custom_call" | custom-call | tf_op jit(solution)/shard_map/adapter_step/pallas_call | solution.py:505
  39.3 1.3 %finish.1 = (bf16[512,1024]{1,0:T(8,128)(2,1)}, bf16[512,512]{1,0:T(8,128)(2,1)}, f32[2,512]{1,0:T(2,128)}, f32[2,64]{1,0:T(2,128)}) custom-call(bf16[2,512,512]{2,1,0:T(8,128)(2,1)S(1)} %get-tuple-element.14.m_ref, bf16[64,512]{1,0:T(8,128)(2,1)S(1)} %get-tuple-element.15.ld_ref, bf16[64,1024]{1,0:T(8,128)(2,1)S(1)} %get-tuple-element.16.nut_ref, ...), custom_call_target="tpu_custom_call" | custom-call | tf_op jit(solution)/shard_map/finish/pallas_call | solution.py:539
